TPU v7x, 512 devices: a whole 4x8x8 slice. The times are simulated.
512 devices in a mesh: ctx: 64 (over z, x, y_hi), head: 8 (over y_lo, core).
Axes of the slice: x: 4, y: 8 (y_hi: 2, y_lo: 4; y = y_hi * 4 + y_lo), z: 8, core: 2. Of those that a mesh axis runs over, the one named last changes fastest.
Arguments:
- query_raw: bfloat16 [8192, 8192], P('ctx', 'head'), may hold values from -6 to 6
- key_before_norm: bfloat16 [8192, 1024], P('ctx', 'head'), may hold values from -6 to 6
- values: bfloat16 [8192, 1024], P('ctx', 'head'), may hold values from -6 to 6
- attention_output_gradient: bfloat16 [8192, 8192], P('ctx', 'head'), may hold values from -6 to 6
- q_gain: float32 [128], replicated, may hold values from 0.5 to 1.5
- k_gain: float32 [128], replicated, may hold values from 0.5 to 1.5
- tok_pos: int32 [8192], P('ctx'), may hold values from 0 to 8191, as said below
Outputs:
- grad_query_raw: bfloat16 [8192, 8192], P('ctx', 'head')
- grad_key_raw: bfloat16 [8192, 1024], P('ctx', 'head')
- value_gradient_rows: bfloat16 [8192, 1024], P('ctx', 'head')
- query_norm_gain_gradient: float32 [128], replicated
- key_norm_gain_gradient: float32 [128], replicated
Inputs may be any that keep to these rules, and one draw needn't show every extreme that they name: `tok_pos`: each position appears once. The rows of one device are two runs of 64 consecutive positions in ascending order: run number p and run number 8192 / 64 - 1 - p, where p differs from device to device.
All inputs are finite; a program needn't handle non-finite values.
Results may differ from a plain program's by a relative error of at most 0.0099.
Values may be sent and summed in bfloat16 or wider, within the bound.
A program may use at most 64 MiB of HBM per device.

v0:
```python
import jax
import jax.numpy as jnp
from jax import lax
from jax.sharding import PartitionSpec as P

HEAD_SIZE = 128


norm_epsilon = 1e-06
rope_base = 1000000.0


def from_behind(value, axis, steps):
    count = lax.axis_size(axis)
    pairs = [(source, (source + steps) % count) for source in range(count)]
    return lax.ppermute(value, axis, pairs)


def rope_tables(positions, width):
    half_width = width // 2
    exponent = jnp.arange(half_width, dtype=jnp.float32) * (2.0 / width)
    frequency = jnp.power(jnp.float32(rope_base), -exponent)
    angles = positions.astype(jnp.float32)[:, None] * frequency[None, :]
    return (jnp.cos(angles)[:, None, :], jnp.sin(angles)[:, None, :])


def rotate(values_in, cosine, sine_table):
    half_width = values_in.shape[-1] // 2
    first_half = values_in[..., :half_width]
    second_half = values_in[..., half_width:]
    return jnp.concatenate(
        [
            first_half * cosine - second_half * sine_table,
            second_half * cosine + first_half * sine_table,
        ],
        axis=-1,
    )


def unrotate(incoming, cosine, sine_table):
    half_width = incoming.shape[-1] // 2
    first_half = incoming[..., :half_width]
    second_half = incoming[..., half_width:]
    return jnp.concatenate(
        [
            first_half * cosine + second_half * sine_table,
            second_half * cosine - first_half * sine_table,
        ],
        axis=-1,
    )


def apply_norm_forward(raw_heads):
    inverse = lax.rsqrt(jnp.mean(raw_heads * raw_heads, axis=-1, keepdims=True) + norm_epsilon)
    return (raw_heads * inverse, inverse)


def norm_backward(incoming, normed, inverse, gain_vector):
    scaled = incoming * gain_vector
    grad_raw = inverse * (scaled - normed * jnp.mean(scaled * normed, axis=-1, keepdims=True))
    grad_gain = jnp.sum(incoming * normed, axis=(0, 1))
    return (grad_raw, grad_gain)


def repeat_steps(advance, steps_count, carried):

    def twice(turn_number, current):
        return advance(advance(current))

    carried = lax.fori_loop(0, steps_count // 2, twice, carried)
    carried = advance(carried)
    return carried


def keep_same(current):
    return current


def shards(query_raw, key_before_norm, values, attention_output_gradient, q_gain, k_gain, tok_pos):
    row_count = query_raw.shape[0]
    half_rows = row_count // 2
    kv_heads = key_before_norm.shape[1] // HEAD_SIZE
    q_heads = query_raw.shape[1] // HEAD_SIZE
    queries_per_group = q_heads // kv_heads
    score_scale = HEAD_SIZE ** (-0.5)
    ctx_count = lax.axis_size("ctx")
    ctx_index = lax.axis_index("ctx")
    cosine, sine_table = rope_tables(tok_pos, HEAD_SIZE)
    q_normed, q_inverse = apply_norm_forward(
        query_raw.astype(jnp.float32).reshape(row_count, q_heads, HEAD_SIZE)
    )
    query_rotated = rotate(q_normed * q_gain, cosine, sine_table).astype(jnp.bfloat16)
    key_after_norm, key_inverse_norm = apply_norm_forward(
        key_before_norm.astype(jnp.float32).reshape(row_count, kv_heads, HEAD_SIZE)
    )
    k_rot = (
        rotate(key_after_norm * k_gain, cosine, sine_table)
        .astype(jnp.bfloat16)
        .reshape(row_count, kv_heads * HEAD_SIZE)
    )

    def by_halves(heads_rows):
        arranged = heads_rows.reshape(
            2, half_rows, kv_heads, queries_per_group, HEAD_SIZE
        ).transpose(0, 2, 3, 1, 4)
        return arranged.reshape(2, kv_heads, queries_per_group * half_rows, HEAD_SIZE)

    q_halves = by_halves(query_rotated)
    g_halves = by_halves(attention_output_gradient.reshape(row_count, q_heads, HEAD_SIZE))
    pos_halves = jnp.tile(tok_pos.reshape(2, 1, half_rows), (1, queries_per_group, 1)).reshape(
        2, queries_per_group * half_rows
    )
    pos_top = jnp.max(tok_pos.reshape(2, half_rows), axis=1)
    key_all, value_all, pos_all = (
        lax.all_gather(k_rot, "ctx", axis=0, tiled=True),
        lax.all_gather(values, "ctx", axis=0, tiled=True),
        lax.all_gather(tok_pos, "ctx", axis=0, tiled=True),
    )
    span_count = key_all.shape[0] // half_rows
    key_spans = key_all.reshape(span_count, half_rows, kv_heads, HEAD_SIZE).transpose(0, 2, 1, 3)
    value_spans = value_all.reshape(span_count, half_rows, kv_heads, HEAD_SIZE).transpose(
        0, 2, 1, 3
    )
    pos_spans = pos_all.reshape(span_count, half_rows)

    def stat_adder(query_half, key_part, value_part, pos_part):

        def stat_add_tile(current):
            scores = (
                jnp.einsum(
                    "kqd,knd->kqn",
                    q_halves[query_half],
                    key_part,
                    preferred_element_type=jnp.float32,
                )
                * score_scale
            )
            visible = pos_part[None, None, :] <= pos_halves[query_half][None, :, None]
            exp_scores = jnp.where(visible, jnp.exp(scores), 0.0)
            grad_probs = jnp.einsum(
                "kqd,knd->kqn", g_halves[query_half], value_part, preferred_element_type=jnp.float32
            )
            return (
                current[0] + jnp.sum(exp_scores, axis=-1),
                current[1] + jnp.sum(exp_scores * grad_probs, axis=-1),
            )

        return stat_add_tile

    per_turn = 8
    turn_count = span_count // per_turn

    def stat_turn(running, entries):
        key_group, value_group, pos_group = entries
        running = list(running)
        for slot_index in range(per_turn):
            for query_half in range(2):
                running[query_half] = lax.cond(
                    jnp.min(pos_group[slot_index]) <= pos_top[query_half],
                    stat_adder(
                        query_half,
                        key_group[slot_index],
                        value_group[slot_index],
                        pos_group[slot_index],
                    ),
                    keep_same,
                    running[query_half],
                )
        return (tuple(running), None)

    stat_zero = jnp.zeros((kv_heads, queries_per_group * half_rows), jnp.float32)
    grouped = (
        key_spans.reshape(turn_count, per_turn, kv_heads, half_rows, HEAD_SIZE),
        value_spans.reshape(turn_count, per_turn, kv_heads, half_rows, HEAD_SIZE),
        pos_spans.reshape(turn_count, per_turn, half_rows),
    )
    stats_done, ignored = lax.scan(
        stat_turn, ((stat_zero, stat_zero), (stat_zero, stat_zero)), grouped
    )
    log_total = [jnp.log(stats_done[query_half][0]) for query_half in range(2)]
    delta_rows = [stats_done[query_half][1] / stats_done[query_half][0] for query_half in range(2)]

    def grad_adder(query_half, key_part, value_part, pos_part):

        def grad_add_tile(current):
            scores = (
                jnp.einsum(
                    "kqd,knd->kqn",
                    q_halves[query_half],
                    key_part,
                    preferred_element_type=jnp.float32,
                )
                * score_scale
            )
            visible = pos_part[None, None, :] <= pos_halves[query_half][None, :, None]
            softmax_probs = jnp.where(
                visible, jnp.exp(scores - log_total[query_half][..., None]), 0.0
            )
            grad_probs = jnp.einsum(
                "kqd,knd->kqn", g_halves[query_half], value_part, preferred_element_type=jnp.float32
            )
            grad_scores = softmax_probs * (grad_probs - delta_rows[query_half][..., None])
            probs_round = softmax_probs.astype(jnp.bfloat16)
            scores_round = grad_scores.astype(jnp.bfloat16)
            grad_query = (
                jnp.einsum(
                    "kqn,knd->kqd", scores_round, key_part, preferred_element_type=jnp.float32
                )
                * score_scale
            )
            grad_key = (
                jnp.einsum(
                    "kqn,kqd->knd",
                    scores_round,
                    q_halves[query_half],
                    preferred_element_type=jnp.float32,
                )
                * score_scale
            )
            value_gradient_head = jnp.einsum(
                "kqn,kqd->knd",
                probs_round,
                g_halves[query_half],
                preferred_element_type=jnp.float32,
            )
            return (
                current[0] + grad_query,
                current[1] + grad_key,
                current[2] + value_gradient_head,
            )

        return grad_add_tile

    def grads_at(block_index):
        wrapped = (block_index + 2 * ctx_count) % ctx_count
        key_pair = lax.dynamic_slice_in_dim(key_spans, wrapped * 2, 2, 0)
        value_pair = lax.dynamic_slice_in_dim(value_spans, wrapped * 2, 2, 0)
        pos_pair = lax.dynamic_slice_in_dim(pos_spans, wrapped * 2, 2, 0)
        query_acc = [
            jnp.zeros((kv_heads, queries_per_group * half_rows, HEAD_SIZE), jnp.float32)
            for query_half in range(2)
        ]
        key_out = []
        value_out = []
        for key_half in range(2):
            key_acc = jnp.zeros((kv_heads, half_rows, HEAD_SIZE), jnp.float32)
            value_acc = jnp.zeros((kv_heads, half_rows, HEAD_SIZE), jnp.float32)
            for query_half in range(2):
                query_acc[query_half], key_acc, value_acc = lax.cond(
                    jnp.min(pos_pair[key_half]) <= pos_top[query_half],
                    grad_adder(
                        query_half, key_pair[key_half], value_pair[key_half], pos_pair[key_half]
                    ),
                    keep_same,
                    (query_acc[query_half], key_acc, value_acc),
                )
            key_out.append(key_acc)
            value_out.append(value_acc)
        return (jnp.stack(query_acc), jnp.stack(key_out), jnp.stack(value_out))

    acc_zero = jnp.zeros((2, kv_heads, half_rows, HEAD_SIZE), jnp.float32)

    def sweep_down(steps_count, query_total):

        def advance(current):
            turn_index, query_sum, key_sum, value_sum = current
            add_query, add_key, add_value = grads_at(ctx_index - steps_count + turn_index)
            key_sum, value_sum = from_behind((key_sum + add_key, value_sum + add_value), "ctx", -1)
            return (turn_index + 1, query_sum + add_query, key_sum, value_sum)

        return repeat_steps(advance, steps_count, (jnp.int32(0), query_total, acc_zero, acc_zero))

    own_query, own_key, own_value = grads_at(ctx_index)
    downward = sweep_down(ctx_count - 1, own_query)
    query_total = downward[1]
    key_total = own_key + downward[2]
    value_total = own_value + downward[3]
    grad_q_rot = (
        query_total.reshape(2, kv_heads, queries_per_group, half_rows, HEAD_SIZE)
        .transpose(0, 3, 1, 2, 4)
        .reshape(row_count, q_heads, HEAD_SIZE)
    )
    grad_k_rot = key_total.transpose(0, 2, 1, 3).reshape(row_count, kv_heads, HEAD_SIZE)
    grad_v_out = (
        value_total.transpose(0, 2, 1, 3)
        .reshape(row_count, kv_heads * HEAD_SIZE)
        .astype(jnp.bfloat16)
    )
    query_norm_backward, q_gain_part = norm_backward(
        unrotate(grad_q_rot, cosine, sine_table), q_normed, q_inverse, q_gain
    )
    key_norm_backward, k_gain_part = norm_backward(
        unrotate(grad_k_rot, cosine, sine_table), key_after_norm, key_inverse_norm, k_gain
    )
    q_gain_sum, k_gain_sum = lax.psum((q_gain_part, k_gain_part), ("ctx", "head"))
    return (
        query_norm_backward.reshape(row_count, q_heads * HEAD_SIZE).astype(jnp.bfloat16),
        key_norm_backward.reshape(row_count, kv_heads * HEAD_SIZE).astype(jnp.bfloat16),
        grad_v_out,
        q_gain_sum,
        k_gain_sum,
    )


def solution(mesh):
    placed = (
        P("ctx", "head"),
        P("ctx", "head"),
        P("ctx", "head"),
        P("ctx", "head"),
        P(),
        P(),
        P("ctx"),
    )
    return jax.shard_map(
        shards,
        mesh=mesh,
        in_specs=placed,
        out_specs=(P("ctx", "head"), P("ctx", "head"), P("ctx", "head"), P(), P()),
        check_vma=False,
    )
```

profile of v0, /device:TPU:1, one launch (start us, length us, event | category | flops | bytes accessed | tf_op | source)
XLA Modules:
  0.0 2294.4 jit_solution(12174564827345355645)
XLA Ops:
  13.2 201.2 %all-gather = s32[64,1,128]{2,1,0:T(1,128)S(1)} all-gather(s32[1,1,128]{2,1,0:T(1,128)} %bitcast.1275), channel_id=1, replica_groups=mesh['ctx'=64,'head'=8] {'ctx'}, dimensions={0}, use_global_device_ids=true | all-gather | bytes 33280 | tf_op jit(solution)/shard_map/all_gather | solution.py:117
  228.9 53.2 %all-gather.4.cloned.1.call-done = bf16[8192,128]{1,0:T(8,128)(2,1)} async-done(((bf16[128,128]{1,0:T(8,128)(2,1)}), bf16[8192,128]{1,0:T(8,128)(2,1)}) %all-gather.4.cloned.1.call-update) | async-done | bytes 2097168 | tf_op jit(solution)/shard_map/all_gather | solution.py:115
  282.9 437.1 %while.40 = (s32[]{:T(128)}, f32[1,512]{1,0:T(1,128)S(1)}, f32[1,512]{1,0:T(1,128)S(1)}, f32[1,512]{1,0:T(1,128)S(1)}, f32[1,512]{1,0:T(1,128)S(1)}, /*index=5*/...) while((s32[]{:T(128)}, f32[1,512]{1,0:T(1,128)S(1)}, ...), condition=%wide.region_78.79_spmd.clone, body=%wide.region_5.78_spmd.clone.sunk | while | flops 271581696 | bytes 9828845 | solution.py:177
  724.8 1372.0 %while.41 = (s32[]{:T(128)}, f32[2,1,512,128]{3,2,1,0:T(8,128)S(1)}, f32[2,1,64,128]{3,2,1,0:T(8,128)S(1)}, f32[2,1,64,128]{3,2,1,0:T(8,128)S(1)}, s32[]{:T(128)...) while((s32[]{:T(128)}, ...), condition=%wide.region_108.109_spmd.clone, body=%wide.region_87.108_spmd.clone.sunk | while | flops 339214624 | bytes 17555340 | solution.py:70
  778.5 10.9 collective-permute-start.2
  864.6 12.4 collective-permute-start.2
  913.3 8.4 collective-permute-start.2
  1088.7 8.8 collective-permute-start.2
  1134.1 8.7 collective-permute-start.2
  1177.1 9.9 collective-permute-start.2
  1220.9 10.1 collective-permute-start.2
  1241.3 8.3 collective-permute-start.3
  1288.1 9.0 collective-permute-start.3
  1356.7 8.0 collective-permute-start.2
  1402.6 8.5 collective-permute-start.2
  1443.9 9.3 collective-permute-start.2
  1531.3 11.2 collective-permute-start.2
  1680.5 9.1 collective-permute-start.3
  1773.7 8.6 collective-permute-start.3
  1843.4 12.2 collective-permute-start.2
  1865.9 7.9 collective-permute-start.3
  2034.5 8.4 collective-permute-start.3
  2108.7 8.9 collective-permute-start.4
  2123.3 163.5 %all-reduce = (f32[128]{0:T(128)}, f32[128]{0:T(128)}) all-reduce(f32[128]{0:T(128)S(1)} %bitcast_reduce_fusion, f32[128]{0:T(128)S(1)} %get-tuple-element.1945), channel_id=1, replica_groups=mesh['ctx'=64,'head'=8] {'ctx','head'}, use_global_device_ids=true, to_apply=%region_123.124 | all-reduce | flops 256 | bytes 2048 | tf_op jit(solution)/shard_map/psum | solution.py:295
  (3233 shorter events, 1259.2 us)
Async XLA Ops:
  7.2 221.0 %all-gather.6.cloned.1.call-start = ((), (), s32[]{:S(2)}) async-start(), calls=%async_computation.1 | async-start | bytes 2129920 | tf_op jit(solution)/shard_map/all_gather | solution.py:116
  7.9 274.2 %all-gather.4.cloned.1.call-start = ((), (), s32[]{:S(2)}) async-start(), calls=%async_computation | async-start | bytes 2129920 | tf_op jit(solution)/shard_map/all_gather | solution.py:115
  735.4 20.7 collective-permute-start.2
  778.5 21.2 collective-permute-start.2
  823.3 19.9 collective-permute-start.2
  864.6 22.6 collective-permute-start.2
  913.3 18.6 collective-permute-start.2
  1006.4 18.9 collective-permute-start
  1088.7 20.2 collective-permute-start.2
  1134.1 18.9 collective-permute-start.2
  1177.1 20.2 collective-permute-start.2
  1220.9 20.4 collective-permute-start.2
  1275.9 21.2 collective-permute-start
  1356.7 20.1 collective-permute-start.2
  1402.6 18.7 collective-permute-start.2
  1443.9 19.5 collective-permute-start.2
  1531.3 21.5 collective-permute-start.2
  1582.6 19.2 collective-permute-start
  1670.2 19.4 collective-permute-start
  1753.7 20.0 collective-permute-start.2
  1758.7 23.6 %collective-permute-start = (f32[2,1,64,128]{3,2,1,0:T(8,128)S(1)}, f32[2,1,64,128]{3,2,1,0:T(8,128)S(1)}, u32[]{:S(2)}, u32[]{:S(2)}) collective-permute-start(f32[2,1,64,128]{3,2,1,0:T(8,128)S(1)} %maximum_add_fusion.14), channel_id=1, source_target_pairs={{0,504},{8,0},{16,8},{24,16},{32,24},{40,32},{48,40},{56,48},{64,5... | collective-permute-start | bytes 196616 | tf_op jit(solution)/shard_map/while/body/eval_jaxpr/ppermute | solution.py:16
  1843.4 22.4 collective-permute-start.2
  2023.7 19.2 collective-permute-start
  2117.6 169.3 %collective-permute-start.5 = (f32[2,1,64,128]{3,2,1,0:T(8,128)S(1)}, f32[2,1,64,128]{3,2,1,0:T(8,128)S(1)}, u32[]{:S(2)}, u32[]{:S(2)}) collective-permute-start(f32[2,1,64,128]{3,2,1,0:T(8,128)S(1)} %maximum_add_fusion.9), channel_id=1, source_target_pairs={{0,504},{8,0},{16,8},{24,16},{32,24},{40,32},{48,40},{56,48},{64,5... | collective-permute-start | bytes 196616 | tf_op jit(solution)/shard_map/ppermute | solution.py:16
  (249 other events, 5105.1 us)
Sparse Core Ops, SparseCore 0:
  12.4 135.8 all-gather.5
  153.2 128.8 all-gather.3
where the time goes:
time: 2320 us; the launch traced here: 2290 us
  loops' own time  649 us (28%)
  starting transfers between devices  613 us (26%)
  blocking collectives  365 us (16%)
  waiting for transfers between devices  226 us (10%)
  matrix products  213 us (9%)
  local copies, waits for them, and re-layouts  143 us (6%)
  other arithmetic  60.1 us (3%)
  between operations  24.9 us (1%)
    ppermute x126, starting transfers between devices, from_behind(): return lax.ppermute(value, axis, pairs)  613 us
    another operation x1, loops' own time, shards(): lax.scan(stat_turn, ((stat_zero, stat_zero), (stat_zero, stat_zero)), gro...  327 us
    another operation x1, loops' own time, repeat_steps(): carried = lax.fori_loop(0, steps_count // 2, twice, carried)  307 us
    all_gather x1, blocking collectives, shards(): lax.all_gather(tok_pos, 'ctx', axis=0, tiled=True)  201 us
    ppermute x126, waiting for transfers between devices, from_behind(): return lax.ppermute(value, axis, pairs)  172 us
    psum x1, blocking collectives, shards(): lax.psum((q_gain_part, k_gain_part), ('ctx', 'head'))  164 us
    dot_general x129, matrix products, grad_add_tile(): jnp.einsum('kqd,knd->kqn', q_halves[query_half], key_part, preferred_elem...  70 us
    all_gather x1, waiting for transfers between devices, shards(): lax.all_gather(k_rot, 'ctx', axis=0, tiled=True)  53.2 us
  transfers between devices with their start and end apart: 128, of which 45 were waited for; matrix products, arithmetic and copies ran while one was open for 5% of the time, Pallas kernels for 0%

commit v1 on v0

v1 whole, which is shorter than its diff:
```python
import functools

import jax
import jax.numpy as jnp
from jax import lax
from jax.experimental import pallas as pl
from jax.experimental.pallas import tpu as pltpu
from jax.sharding import PartitionSpec as P

D = 128
HALF = 64
X, Y, Z = 4, 2, 8
HEADS = 8
EPS = 1e-06
BASE = 1000000.0
SCALE = D ** (-0.5)
LOG2E = 1.4426950408889634
KROWS = 144
F32, BF16 = jnp.float32, jnp.bfloat16
NT = (((1,), (1,)), ((), ()))
NN = (((1,), (0,)), ((), ()))
TN = (((0,), (0,)), ((), ()))


def dot(a, b, dims):
    return lax.dot_general(a, b, dims, preferred_element_type=F32)


def message_table():
    names = ["YK", "YV", "XKR", "XKL", "XKR2", "XKL2"]
    for way in "RL":
        for step in (1, 2, 3):
            names += [f"ZK{way}{step}{half}" for half in (0, 1)]
        names.append(f"ZK{way}4{1 if way == 'R' else 0}")
        names += [f"ZV{way}{step}" for step in (1, 2, 3, 4)]
    for s in range(8):
        names += [f"XVR{s}", f"XVL{s}", f"XVR2{s}", f"XVL2{s}"]
    for way in "RL":
        names.append(f"RK{way}1{1 if way == 'R' else 0}")
        for step in (2, 3, 4):
            names += [f"RK{way}{step}{half}" for half in (0, 1)]
        names += [f"RV{way}{step}" for step in (1, 2, 3, 4)]
        names += [f"RVX1{way}{t}" for t in range(8)]
        names += [f"RVX2{way}{t}" for t in range(8)]
    names += ["RKX1", "RKX2", "RKX3", "RKY", "RVY"]
    return {name: index for index, name in enumerate(names)}


MSG = message_table()


class Part:
    def __init__(self, ref, index=None):
        self.ref, self.index = ref, index

    def make(self):
        return self.ref if self.index is None else self.ref.at[self.index]

    @property
    def at(self):
        return Maker(self.ref)

    def __getitem__(self, index):
        return self.make()[index]

    def __setitem__(self, index, value):
        self.make()[index] = value


class Maker:
    def __init__(self, ref):
        self.ref = ref

    def __getitem__(self, index):
        return Part(self.ref, index)


def body(
    heads_axis, q_ref, k_ref, v_ref, g_ref, qg_ref, kg_ref, cos_ref, sin_ref, p_ref, swap_ref,
    dq_ref, dk_ref, dv_ref, gain_ref,
    kb, vb, e_a, g_a, e_b, g_b, e_d, g_d, qc, gc, sums, stats, dqacc, dkd, dvd,
    dkb, dvb, rk, rvx1, rvx2, rvz, rkx, rky, rvy, ysend, gbuf, gsum,
    ssem, rsem, gssem, grsem,
):
    kb, vb, dkb, dvb, rk, rvx1, rvx2, rvz, rkx, rky, rvy, ysend = (
        Part(ref) for ref in (kb, vb, dkb, dvb, rk, rvx1, rvx2, rvz, rkx, rky, rvy, ysend)
    )
    ctx = lax.axis_index("ctx")
    head = lax.axis_index("head")
    z, x, y = ctx // (X * Y), (ctx // Y) % X, ctx % Y
    w = ctx % (X * Y)
    oy = 1 - y

    zpos = [lax.rem(z + off, Z) for off in range(Z)]
    xpos = [lax.rem(x + off, X) for off in range(X)]

    def zm(off):
        return zpos[off % Z] if isinstance(off, int) else lax.rem(z + off + Z, Z)

    def xm(off):
        return xpos[off % X]


    def dev(zz, xx, yy):
        return ((zz * X + xx) * Y + yy, head)

    def peers():
        out = []
        for j in range(1, 8):
            out.append((lax.rem(z + j, Z) * (X * Y) + w, head))
        for j in range(1, 8):
            out.append((z * (X * Y) + lax.rem(w + j, X * Y), head))
        for j in range(1, heads_axis):
            out.append((ctx, lax.rem(head + j, heads_axis)))
        return out

    barrier = pltpu.get_barrier_semaphore()
    all_peers = peers()
    for peer in all_peers:
        pl.semaphore_signal(barrier, inc=1, device_id=peer, device_id_type=pl.DeviceIdType.MESH)

    started = []

    def copy(name, src, dst, to):
        i = MSG[name]
        return pltpu.make_async_remote_copy(
            src_ref=src.make(), dst_ref=dst.make(), send_sem=ssem.at[i], recv_sem=rsem.at[i],
            device_id=to, device_id_type=pl.DeviceIdType.MESH,
        )

    def send(name, src, dst, to):
        copy(name, src, dst, to).start()
        started.append((name, src, dst, to))

    def arrived(name, dst):
        copy(name, dst, dst, (ctx, head)).wait_recv()

    right_z, left_z = dev(zm(1), x, y), dev(zm(-1), x, y)
    right_x, left_x = dev(z, xm(1), y), dev(z, xm(-1), y)
    side = {"R": (right_z, -1), "L": (left_z, 1)}

    swapped = swap_ref[0:1, :] > 0.5
    p_me = p_ref[...]

    def halves(v):
        first, second = v[:HALF], v[HALF:]
        return jnp.where(swapped, second, first), jnp.where(swapped, first, second)

    def rope(v):
        return v * cos_ref[...] + pltpu.roll(v, HALF, 1) * sin_ref[...]

    def unrope(v):
        return v * cos_ref[...] - pltpu.roll(v, HALF, 1) * sin_ref[...]

    def normed(v):
        inverse = lax.rsqrt(jnp.mean(v * v, axis=-1, keepdims=True) + EPS)
        return v * inverse, inverse

    kn, _ = normed(k_ref[...].astype(F32))
    k_lo, k_hi = halves(rope(kn * kg_ref[...]))
    v_lo, v_hi = halves(v_ref[...].astype(F32))
    kb[z, x, y, 0:HALF] = k_lo.astype(BF16)
    kb[z, x, y, HALF:D] = k_hi.astype(BF16)
    kb[z, x, y, D:KROWS] = jnp.concatenate([p_me, p_me], axis=0).astype(BF16)
    vb[x, z, y, 0:HALF] = v_lo.astype(BF16)
    vb[x, z, y, HALF:D] = v_hi.astype(BF16)

    pl.semaphore_wait(barrier, len(all_peers))

    partner = dev(z, x, oy)
    send("YV", vb.at[x, z, y], vb.at[x, z, y], partner)
    send("YK", kb.at[z, x, y], kb.at[z, x, y], partner)

    for h in range(HEADS):
        cols = slice(h * D, (h + 1) * D)
        rows = slice(h * HALF, (h + 1) * HALF)
        qn, _ = normed(q_ref[:, cols].astype(F32))
        lo, hi = halves(rope(qn * qg_ref[...]))
        qc[rows, 0:D] = lo.astype(BF16)
        qc[rows, D:] = hi.astype(BF16)
        lo, hi = halves(g_ref[:, cols].astype(F32))
        gc[rows, 0:D] = lo.astype(BF16)
        gc[rows, D:] = hi.astype(BF16)

    arrived("YV", vb.at[x, z, oy])
    for way in "RL":
        to, _ = side[way]
        send(f"ZV{way}1", vb.at[x, z], vb.at[x, z], to)
    arrived("YK", kb.at[z, x, oy])
    send("XKR", kb.at[z, x], kb.at[z, x], right_x)
    send("XKL", kb.at[z, x], kb.at[z, x], left_x)
    send("XVR0", vb.at[x, z], vb.at[x, z], right_x)
    send("XVL0", vb.at[x, z], vb.at[x, z], left_x)

    zero = jnp.zeros((HALF, D), BF16)

    def diagonal(buffer_lo, buffer_hi):
        return jnp.concatenate(
            [
                jnp.concatenate([buffer_lo, zero], axis=1),
                jnp.concatenate([zero, buffer_hi], axis=1),
            ],
            axis=0,
        )

    def own_k():
        return diagonal(kb[z, x, y, 0:HALF], kb[z, x, y, HALF:D])

    def own_v():
        return diagonal(vb[x, z, y, 0:HALF], vb[x, z, y, HALF:D])

    scores = dot(own_k(), qc[...], NT)
    key_row = lax.broadcasted_iota(jnp.int32, (D, 8 * HALF), 0) % HALF
    query_lane = lax.broadcasted_iota(jnp.int32, (D, 8 * HALF), 1) % HALF
    exps = jnp.where(key_row <= query_lane, jnp.exp2(scores * (SCALE * LOG2E)), 0.0)
    probs_grad = dot(own_v(), gc[...], NT)
    e_d[...] = exps
    g_d[...] = probs_grad
    both = exps * probs_grad
    for part in range(2):
        rows = slice(part * HALF, (part + 1) * HALF)
        sums[part] = exps[rows].reshape(8, 8, 8 * HALF).sum(0)
        sums[2 + part] = both[rows].reshape(8, 8, 8 * HALF).sum(0)

    arrived("XKR", kb.at[z, xm(-1)])
    send("XKR2", kb.at[z, xm(-1), 0], kb.at[z, xm(-1), 0], right_x)
    arrived("XKL", kb.at[z, xm(1)])
    send("XKL2", kb.at[z, xm(1), 1], kb.at[z, xm(1), 1], left_x)
    arrived("XKR2", kb.at[z, xm(2), 0])
    arrived("XKL2", kb.at[z, xm(2), 1])

    def kpart(zz, half):
        return kb.at[zz, pl.ds(2 * half, 2)]

    for half in range(2):
        for way in "RL":
            to, _ = side[way]
            send(f"ZK{way}1{half}", kpart(z, half), kpart(z, half), to)

    def offset_of(s):
        h = (s + 1) // 2
        return h * (1 - 2 * (s % 2))

    def v_progress(s):
        if s == 0:
            for way, nb in (("R", -1), ("L", 1)):
                arrived(f"XV{way}0", vb.at[xm(nb), z])
                pick = 0 if way == "R" else 1
                src = vb.at[xm(nb), z, pick]
                send(f"XV{way}20", src, src, right_x if way == "R" else left_x)
        d = s + 1
        if d <= 4:
            for way in "RL":
                to, sign = side[way]
                src = zm(sign * d)
                if d < 4:
                    arrived(f"ZV{way}{d}", vb.at[x, src])
                    nxt = vb.at[x, src]
                    if d == 3:
                        nxt = vb.at[x, src, 1 if way == "R" else 0]
                    send(f"ZV{way}{d + 1}", nxt, nxt, to)
                    c = 2 * d - 1 if way == "R" else 2 * d
                    send(f"XVR{c}", vb.at[x, src], vb.at[x, src], right_x)
                    send(f"XVL{c}", vb.at[x, src], vb.at[x, src], left_x)
                else:
                    arrived(f"ZV{way}4", vb.at[x, src, 1 if way == "R" else 0])
            if d == 4:
                src = vb.at[x, zm(4)]
                send("XVR7", src, src, right_x)
                send("XVL7", src, src, left_x)
        if s < 7:
            c = s + 1
            zz = zm(offset_of(c))
            for way, nb in (("R", -1), ("L", 1)):
                arrived(f"XV{way}{c}", vb.at[xm(nb), zz])
                src = vb.at[xm(nb), zz, 0 if way == "R" else 1]
                send(f"XV{way}2{c}", src, src, right_x if way == "R" else left_x)
        zz = zm(offset_of(s))
        arrived(f"XVR2{s}", vb.at[xm(2), zz, 0])
        arrived(f"XVL2{s}", vb.at[xm(2), zz, 1])

    def k_progress(s, half):
        if s == 0:
            return
        d = (s + 1) // 2
        if s < 7:
            way = "R" if s % 2 else "L"
            to, sign = side[way]
            src = kpart(zm(sign * d), half)
            arrived(f"ZK{way}{d}{half}", src)
            if d < 3 or half == (1 if way == "R" else 0):
                send(f"ZK{way}{d + 1}{half}", src, src, to)
        else:
            way = "R" if half == 1 else "L"
            arrived(f"ZK{way}4{half}", kpart(zm(4), half))

    def block_masks(zz, half):
        pj = kb[zz, pl.ds(2 * half, 2), :, D:KROWS, :].reshape(4, 16, D).astype(F32)[:, 0:8, :]
        early = jnp.where(pj < p_me[None], 1.0, 0.0)
        other = jnp.where(pj == p_me[None], 0.0, 1.0)
        return early, other

    def wide(v):
        return jnp.concatenate([v, v, v, v], axis=-1)

    def lows(buffer):
        return buffer[0].reshape(4, HALF, D), buffer[1].reshape(4, HALF, D)

    def k_halves(zz, half):
        return (
            kb[zz, pl.ds(2 * half, 2), :, 0:HALF, :].reshape(4, HALF, D),
            kb[zz, pl.ds(2 * half, 2), :, HALF:D, :].reshape(4, HALF, D),
        )

    def v_halves(zz, half):
        return (
            vb[pl.ds(2 * half, 2), zz, :, 0:HALF, :].reshape(4, HALF, D),
            vb[pl.ds(2 * half, 2), zz, :, HALF:D, :].reshape(4, HALF, D),
        )

    def joined(lo, hi, early):
        e = early[:, 0:1, :].astype(BF16)
        return jnp.concatenate([lo * e, hi * (1.0 - e).astype(BF16)], axis=-1).reshape(4 * HALF, 2 * D)

    def pass_one(s, half, u):
        zz = zm(offset_of(s))
        early, other = block_masks(zz, half)
        klo, khi = k_halves(zz, half)
        vlo, vhi = v_halves(zz, half)
        ex = jnp.exp2(dot(klo.reshape(4 * HALF, D), qc[:, D:], NT) * (SCALE * LOG2E))
        gp = dot(vlo.reshape(4 * HALF, D), gc[:, D:], NT)
        e_a[u] = ex
        g_a[u] = gp
        sums[1] += ex.reshape(32, 8, 8 * HALF).sum(0)
        sums[3] += (ex * gp).reshape(32, 8, 8 * HALF).sum(0)
        ex = jnp.exp2(dot(joined(klo, khi, early), qc[...], NT) * (SCALE * LOG2E))
        ex = (ex.reshape(4, HALF, 8 * HALF) * wide(other[:, 0:1, :]))
        gp = dot(joined(vlo, vhi, early), gc[...], NT).reshape(4, HALF, 8 * HALF)
        e_b[u] = ex.reshape(4 * HALF, 8 * HALF)
        g_b[u] = gp.reshape(4 * HALF, 8 * HALF)
        part = ex.reshape(4, 8, 8, 8 * HALF).sum(1)
        partg = (ex * gp).reshape(4, 8, 8, 8 * HALF).sum(1)
        ew = wide(early)
        sums[0] += (part * ew).sum(0)
        sums[1] += (part * (1.0 - ew)).sum(0)
        sums[2] += (partg * ew).sum(0)
        sums[3] += (partg * (1.0 - ew)).sum(0)

    def first_loop(u, carry):
        s, half = u // 2, u % 2
        for case in range(16):
            @pl.when(u == case)
            def _(case=case):
                if case % 2 == 0:
                    v_progress(case // 2)
                k_progress(case // 2, case % 2)
        pass_one(s, half, u)
        return carry

    lax.fori_loop(0, 16, first_loop, 0)

    for part in range(2):
        inv = 1.0 / jnp.sum(sums[part], axis=0, keepdims=True)
        stats[part] = jnp.broadcast_to(inv, (8, 8 * HALF))
        stats[2 + part] = jnp.broadcast_to(
            jnp.sum(sums[2 + part], axis=0, keepdims=True) * inv, (8, 8 * HALF)
        )

    rowsel = lax.broadcasted_iota(jnp.int32, (D, 8 * HALF), 0) < HALF
    pr = e_d[...] * jnp.where(rowsel, stats[0, 0:1], stats[1, 0:1])
    gs = (pr * (g_d[...] - jnp.where(rowsel, stats[2, 0:1], stats[3, 0:1]))).astype(BF16)
    pr = pr.astype(BF16)
    top = lax.broadcasted_iota(jnp.int32, (D, D), 0) < HALF
    full = dot(pr, gc[...], NN)
    dvd[...] = jnp.where(top, full[:, 0:D], full[:, D:])
    full = dot(gs, qc[...], NN)
    dkd[...] = jnp.where(top, full[:, 0:D], full[:, D:]) * SCALE
    dqacc[...] = dot(own_k(), gs, TN)

    def pass_two(s, half, u):
        zz = zm(offset_of(s))
        early, _ = block_masks(zz, half)
        klo, khi = k_halves(zz, half)
        pr = e_a[u] * stats[1, 0:1]
        gs = (pr * (g_a[u] - stats[3, 0:1])).astype(BF16)
        pr = pr.astype(BF16)
        dva = dot(pr, gc[:, D:], NN).reshape(4, HALF, D)
        dka = dot(gs, qc[:, D:], NN).reshape(4, HALF, D)
        dqacc[D:, :] += dot(klo.reshape(4 * HALF, D), gs, TN)
        ew = wide(early[:, 0:1, :]) > 0.5
        invb = jnp.where(ew, stats[0, 0:1][None], stats[1, 0:1][None])
        delb = jnp.where(ew, stats[2, 0:1][None], stats[3, 0:1][None])
        pr = e_b[u].reshape(4, HALF, 8 * HALF) * invb
        gs = (pr * (g_b[u].reshape(4, HALF, 8 * HALF) - delb)).astype(BF16).reshape(4 * HALF, 8 * HALF)
        pr = pr.astype(BF16).reshape(4 * HALF, 8 * HALF)
        dvc = dot(pr, gc[...], NN).reshape(4, HALF, 2 * D)
        dkc = dot(gs, qc[...], NN).reshape(4, HALF, 2 * D)
        dqacc[...] += dot(joined(klo, khi, early), gs, TN)
        e1 = early[:, 0:1, :]
        pair = pl.ds(2 * half, 2)
        shape = (2, 2, HALF, D)
        dkb[zz, pair, :, 0:HALF, :] = ((dka + dkc[..., 0:D] * e1) * SCALE).astype(BF16).reshape(shape)
        dkb[zz, pair, :, HALF:D, :] = (dkc[..., D:] * ((1.0 - e1) * SCALE)).astype(BF16).reshape(shape)
        dvb[zz, pair, :, 0:HALF, :] = (dva + dvc[..., 0:D] * e1).astype(BF16).reshape(shape)
        dvb[zz, pair, :, HALF:D, :] = (dvc[..., D:] * (1.0 - e1)).astype(BF16).reshape(shape)

    def added(ref, *others):
        total = ref[...].astype(F32)
        for other in others:
            total = total + other[...].astype(F32)
        return total

    def add_into(ref, *others):
        ref[...] = added(ref, *others).astype(BF16)

    def dkpart(zz, half):
        return dkb.at[zz, pl.ds(2 * half, 2)]

    def k_reduce(t, half):
        s = 7 - t
        off = offset_of(s)
        zz = zm(off)
        part = dkpart(zz, half)
        if t == 0:
            wi, way = (0, "R") if half == 1 else (1, "L")
            send(f"RK{way}1{half}", part, rk.at[wi, 0, half], side[way][0])
        elif t < 7:
            way = "R" if off > 0 else "L"
            wi = 0 if way == "R" else 1
            step = 4 - abs(off)
            if step > 1 or half == (1 if way == "R" else 0):
                arrived(f"RK{way}{step}{half}", rk.at[wi, step - 1, half])
                add_into(part, rk.at[wi, step - 1, half])
            send(f"RK{way}{step + 1}{half}", part, rk.at[wi, step, half], side[way][0])
        else:
            for wi, way in enumerate("RL"):
                arrived(f"RK{way}4{half}", rk.at[wi, 3, half])
            add_into(part, rk.at[0, 3, half], rk.at[1, 3, half])

    def v_reduce(t):
        if t < 8:
            zz = zm(offset_of(7 - t))
            send(f"RVX1R{t}", dvb.at[zz, xm(2), 0], rvx1.at[0, t], right_x)
            send(f"RVX1L{t}", dvb.at[zz, xm(2), 1], rvx1.at[1, t], left_x)
        if 1 <= t <= 8:
            c = t - 1
            zz = zm(offset_of(7 - c))
            arrived(f"RVX1R{c}", rvx1.at[0, c])
            add_into(dvb.at[zz, xm(1), 0], rvx1.at[0, c])
            send(f"RVX2R{c}", dvb.at[zz, xm(1)], rvx2.at[0, c], right_x)
            arrived(f"RVX1L{c}", rvx1.at[1, c])
            add_into(dvb.at[zz, xm(-1), 1], rvx1.at[1, c])
            send(f"RVX2L{c}", dvb.at[zz, xm(-1)], rvx2.at[1, c], left_x)
        if 2 <= t <= 9:
            c = t - 2
            off = offset_of(7 - c)
            zz = zm(off)
            arrived(f"RVX2R{c}", rvx2.at[0, c])
            arrived(f"RVX2L{c}", rvx2.at[1, c])
            if c == 0:
                add_into(dvb.at[zz, x], rvx2.at[0, c], rvx2.at[1, c])
                send("RVR1", dvb.at[zz, x, 1], rvz.at[0, 0, 1], right_z)
                send("RVL1", dvb.at[zz, x, 0], rvz.at[1, 0, 0], left_z)
            elif c < 7:
                way = "R" if off > 0 else "L"
                wi = 0 if way == "R" else 1
                step = 4 - abs(off)
                add_into(dvb.at[zz, x], rvx2.at[0, c], rvx2.at[1, c])
                if step == 1:
                    side_half = 1 if way == "R" else 0
                    arrived(f"RV{way}1", rvz.at[wi, 0, side_half])
                    add_into(dvb.at[zz, x, side_half], rvz.at[wi, 0, side_half])
                else:
                    arrived(f"RV{way}{step}", rvz.at[wi, step - 1])
                    add_into(dvb.at[zz, x], rvz.at[wi, step - 1])
                send(f"RV{way}{step + 1}", dvb.at[zz, x], rvz.at[wi, step], side[way][0])
            else:
                arrived("RVR4", rvz.at[0, 3])
                arrived("RVL4", rvz.at[1, 3])
                add_into(dvb.at[zz, x], rvx2.at[0, c], rvx2.at[1, c], rvz.at[0, 3], rvz.at[1, 3])

    def second_loop(i, carry):
        t, half = i // 2, i % 2
        s = 7 - t
        pass_two(s, half, 2 * s + half)
        for case in range(16):
            @pl.when(i == case)
            def _(case=case):
                k_reduce(case // 2, case % 2)
                if case % 2 == 1:
                    v_reduce(case // 2)
        return carry

    lax.fori_loop(0, 16, second_loop, 0)
    for j in (1, 2, 3):
        send(f"RKX{j}", dkb.at[z, xm(j)], rkx.at[j - 1], dev(z, xm(j), y))
    v_reduce(8)

    def stored(lo, hi):
        return jnp.concatenate(
            [jnp.where(swapped, hi, lo), jnp.where(swapped, lo, hi)], axis=0
        )

    def norm_back(g, xn, inverse, gain):
        s = g * gain
        return inverse * (s - xn * jnp.mean(s * xn, axis=-1, keepdims=True))

    turned = jnp.transpose(dqacc[...]) * SCALE
    gain_sum = jnp.zeros((1, D), F32)
    for h in range(HEADS):
        cols = slice(h * D, (h + 1) * D)
        rows = slice(h * HALF, (h + 1) * HALF)
        gq = unrope(stored(turned[rows, 0:D], turned[rows, D:]))
        qn, inverse = normed(q_ref[:, cols].astype(F32))
        gain_sum = gain_sum + jnp.sum(gq * qn, axis=0, keepdims=True)
        dq_ref[:, cols] = norm_back(gq, qn, inverse, qg_ref[...]).astype(BF16)

    for j in (1, 2, 3):
        arrived(f"RKX{j}", rkx.at[j - 1])
    ysend[0] = added(dkb.at[z, x, oy], rkx.at[0, oy], rkx.at[1, oy], rkx.at[2, oy]).astype(BF16)
    send("RKY", ysend.at[0], rky, partner)
    v_reduce(9)
    send("RVY", dvb.at[z, x, oy], rvy, partner)
    dk_own = added(dkb.at[z, x, y], rkx.at[0, y], rkx.at[1, y], rkx.at[2, y]) + dkd[...]
    arrived("RKY", rky)
    dk_own = dk_own + rky[...].astype(F32)
    gk = unrope(stored(dk_own[:HALF], dk_own[HALF:]))
    kn, inverse = normed(k_ref[...].astype(F32))
    key_gain = jnp.sum(gk * kn, axis=0, keepdims=True)
    dk_ref[...] = norm_back(gk, kn, inverse, kg_ref[...]).astype(BF16)

    mine = jnp.concatenate([gain_sum, key_gain, jnp.zeros((6, D), F32)], axis=0)
    groups = (
        (z, Z, lambda j: (lax.rem(z + j, Z) * (X * Y) + w, head)),
        (w, X * Y, lambda j: (z * (X * Y) + lax.rem(w + j, X * Y), head)),
        (head, heads_axis, lambda j: (ctx, lax.rem(head + j, heads_axis))),
    )
    for stage, (me, size, peer) in enumerate(groups):
        gsum[stage] = mine
        gbuf[stage, me] = mine
        copies = []
        for j in range(1, size):
            c = pltpu.make_async_remote_copy(
                src_ref=gsum.at[stage], dst_ref=gbuf.at[stage, me],
                send_sem=gssem.at[stage, j], recv_sem=grsem.at[stage, j],
                device_id=peer(j), device_id_type=pl.DeviceIdType.MESH,
            )
            c.start()
            copies.append(c)
        if stage == 0:
            arrived("RVY", rvy)
            dv_own = added(dvb.at[z, x, y], rvy) + dvd[...]
            dv_ref[...] = stored(dv_own[:HALF], dv_own[HALF:]).astype(BF16)
        for c in copies:
            c.wait()
        mine = gbuf[stage, 0]
        for j in range(1, size):
            mine = mine + gbuf[stage, j]
    gain_ref[...] = mine

    for name, src, dst, to in started:
        copy(name, src, dst, to).wait_send()


def shards(heads_axis, query_raw, key_before_norm, values, grads, q_gain, k_gain, tok_pos):
    first, second = tok_pos[0], tok_pos[HALF]
    run = (jnp.minimum(first, second) // HALF).astype(F32)
    p = jnp.full((8, D), run, F32)
    swap = jnp.full((8, D), (first > second).astype(F32), F32)
    frequency = jnp.power(F32(BASE), -(jnp.arange(HALF, dtype=F32) * (2.0 / D)))
    angles = tok_pos.astype(F32)[:, None] * frequency[None, :]
    cosine, sine = jnp.cos(angles), jnp.sin(angles)
    cos2 = jnp.concatenate([cosine, cosine], axis=-1)
    sin2 = jnp.concatenate([-sine, sine], axis=-1)
    vmem = pl.BlockSpec(memory_space=pltpu.VMEM)
    Q = HEADS * HALF
    count = len(MSG)
    dq, dk, dv, gains = pl.pallas_call(
        functools.partial(body, heads_axis),
        out_shape=(
            jax.ShapeDtypeStruct((D, HEADS * D), BF16),
            jax.ShapeDtypeStruct((D, D), BF16),
            jax.ShapeDtypeStruct((D, D), BF16),
            jax.ShapeDtypeStruct((8, D), F32),
        ),
        in_specs=[vmem] * 10,
        out_specs=(vmem,) * 4,
        scratch_shapes=[
            pltpu.VMEM((Z, X, Y, KROWS, D), BF16),
            pltpu.VMEM((X, Z, Y, D, D), BF16),
            pltpu.VMEM((16, 4 * HALF, Q), F32),
            pltpu.VMEM((16, 4 * HALF, Q), F32),
            pltpu.VMEM((16, 4 * HALF, Q), F32),
            pltpu.VMEM((16, 4 * HALF, Q), F32),
            pltpu.VMEM((D, Q), F32),
            pltpu.VMEM((D, Q), F32),
            pltpu.VMEM((Q, 2 * D), BF16),
            pltpu.VMEM((Q, 2 * D), BF16),
            pltpu.VMEM((4, 8, Q), F32),
            pltpu.VMEM((4, 8, Q), F32),
            pltpu.VMEM((2 * D, Q), F32),
            pltpu.VMEM((D, D), F32),
            pltpu.VMEM((D, D), F32),
            pltpu.VMEM((Z, X, Y, D, D), BF16),
            pltpu.VMEM((Z, X, Y, D, D), BF16),
            pltpu.VMEM((2, 4, 2, 2, 2, D, D), BF16),
            pltpu.VMEM((2, 8, D, D), BF16),
            pltpu.VMEM((2, 8, 2, D, D), BF16),
            pltpu.VMEM((2, 4, 2, D, D), BF16),
            pltpu.VMEM((3, 2, D, D), BF16),
            pltpu.VMEM((D, D), BF16),
            pltpu.VMEM((D, D), BF16),
            pltpu.VMEM((1, D, D), BF16),
            pltpu.VMEM((3, 8, 8, D), F32),
            pltpu.VMEM((3, 8, D), F32),
            pltpu.SemaphoreType.DMA((count,)),
            pltpu.SemaphoreType.DMA((count,)),
            pltpu.SemaphoreType.DMA((3, 8)),
            pltpu.SemaphoreType.DMA((3, 8)),
        ],
        compiler_params=pltpu.CompilerParams(
            collective_id=0, has_side_effects=True, vmem_limit_bytes=60 * 1024 * 1024
        ),
    )(
        query_raw, key_before_norm, values, grads,
        q_gain.reshape(1, D), k_gain.reshape(1, D), cos2, sin2, p, swap,
    )
    return dq, dk, dv, gains[0], gains[1]


def solution(mesh):
    split = P("ctx", "head")
    return jax.shard_map(
        functools.partial(shards, mesh.shape["head"]),
        mesh=mesh,
        in_specs=(split, split, split, split, P(), P(), P("ctx")),
        out_specs=(split, split, split, P(), P()),
        check_vma=False,
    )
```

time: 2320 us -> 134 us (0.06); the launches traced: 2290 us -> 134 us
  loops' own time: 649 us -> 0 us
  starting transfers between devices: 613 us -> 0 us
  blocking collectives: 365 us -> 0 us
  waiting for transfers between devices: 226 us -> 0 us
  matrix products: 213 us -> 0 us
  local copies, waits for them, and re-layouts: 143 us -> 6.76 us
  Pallas kernels: 0 us -> 123 us
  other arithmetic: 60.1 us -> 1.07 us
    another operation x514 -> x0, loops' own time: 649 us -> none  [the longest x1 327 us: shards(): lax.scan(stat_turn, ((stat_zero, stat_zero), (stat_zero, stat_zero)), gro...]
    ppermute x126 -> x0, starting transfers between devices: 613 us -> none  [from_behind(): return lax.ppermute(value, axis, pairs)]
    dot_general x903 -> x0, matrix products: 213 us -> none  [the longest x129 70 us: grad_add_tile(): jnp.einsum('kqd,knd->kqn', q_halves[query_half], key_part, preferred_elem...]
    all_gather x1 -> x0, blocking collectives: 201 us -> none  [shards(): lax.all_gather(tok_pos, 'ctx', axis=0, tiled=True)]
    ppermute x126 -> x0, waiting for transfers between devices: 172 us -> none  [from_behind(): return lax.ppermute(value, axis, pairs)]
    psum x1 -> x0, blocking collectives: 164 us -> none  [shards(): lax.psum((q_gain_part, k_gain_part), ('ctx', 'head'))]
    pallas_call x0 -> x1, Pallas kernels: none -> 123 us  [shards(): pl.pallas_call(functools.partial(body, heads_axis), out_shape=(jax.ShapeD...]
    all_gather x2 -> x0, waiting for transfers between devices: 53.2 us -> none  [the longest x1 53.2 us: shards(): lax.all_gather(k_rot, 'ctx', axis=0, tiled=True)]
  transfers between devices with their start and end apart: 128 -> 0, of which waited for: 45 -> 0; matrix products, arithmetic and copies ran while one was open for 5% -> 0% of each run, Pallas kernels for 0% -> 0%
where the time goes in v1:
time: 134 us
  Pallas kernels  123 us (92%)
  local copies, waits for them, and re-layouts  6.76 us (5%)
  between operations  3.28 us (2%)
    pallas_call x1, Pallas kernels, shards(): pl.pallas_call(functools.partial(body, heads_axis), out_shape=(jax.ShapeD...  123 us
    unnamed x9, local copies, waits for them, and re-layouts  3.71 us

profile of v1, /device:TPU:1, one launch (start us, length us, event | category | flops | bytes accessed | tf_op | source)
XLA Modules:
  0.0 133.6 jit_solution(16771384342881474534)
XLA Ops:
  0.6 0.0 copy-start.2
  0.6 0.6 copy-done.2
  1.3 0.6 fusion.1
  4.5 0.6 broadcast_in_dim.8.p_ref
  5.1 0.6 broadcast_in_dim.9.swap_ref
  5.7 0.3 fusion
  6.0 0.7 pad_maximum_fusion
  6.8 122.5 %shard_map.110 = (bf16[128,1024]{1,0:T(8,128)(2,1)}, bf16[128,128]{1,0:T(8,128)(2,1)}, bf16[128,128]{1,0:T(8,128)(2,1)}, f32[8,128]{1,0:T(8,128)}) custom-call(bf16[128,1024]{1,0:T(8,128)(2,1)} %q_ref.1, bf16[128,128]{1,0:T(8,128)(2,1)} %k_ref.1, bf16[128,128]{1,0:T(8,128)(2,1)} %v_ref.1, bf16[128,1024]{1,0:T(8,128)(2,1)} %g_ref.1, f32[1,128]{1,0:T(1,128)} %bitcast.8, ...), custom_call_target="tpu_custom_call" | custom-call | tf_op jit(solution)/shard_map/pallas_call | solution.py:578
  129.3 1.3 slice_bitcast_fusion
  130.6 0.0 copy-start.1
  130.6 1.7 %copy.15 = bf16[128,1024]{1,0:T(8,128)(2,1)} copy(bf16[128,1024]{1,0:T(8,128)(2,1)} %get-tuple-element.27) | data formatting | bytes 524288
  132.2 0.0 copy-done.1
  132.3 0.0 copy-start
  132.3 0.6 copy.16
  132.9 0.2 copy-done
  133.0 0.6 copy.17
  (2 shorter events, 0.0 us)
Async XLA Ops:
  0.6 0.7 copy-start.2
  130.6 1.7 %copy-start.1 = (bf16[128,128]{1,0:T(8,128)(2,1)S(1)}, bf16[128,128]{1,0:T(8,128)(2,1)}, u32[]{:S(2)}) copy-start(bf16[128,128]{1,0:T(8,128)(2,1)} %get-tuple-element.28) | copy-start | bytes 98308
  132.3 0.8 copy-start

commit v2 on v1

v2 whole, which is shorter than its diff:
```python
import functools

import jax
import jax.numpy as jnp
from jax import lax
from jax.experimental import pallas as pl
from jax.experimental.pallas import tpu as pltpu
from jax.sharding import PartitionSpec as P

D = 128
HALF = 64
X, Y, Z = 4, 2, 8
HEADS = 8
Q = HEADS * HALF
EPS = 1e-06
BASE = 1000000.0
SCALE = D ** (-0.5)
LOG2E = 1.4426950408889634
KROWS = 144
F32, BF16 = jnp.float32, jnp.bfloat16
NT = (((1,), (1,)), ((), ()))
NN = (((1,), (0,)), ((), ()))
TN = (((0,), (0,)), ((), ()))


def dot(a, b, dims):
    return lax.dot_general(a, b, dims, preferred_element_type=F32)


def message_table():
    names = ["Y", "QR", "QL", "GR", "GL", "Q2", "G2"]
    for way in "RL":
        for step in (1, 2, 3):
            names += [f"Z{way}{step}{r}" for r in (0, 1)]
        names.append(f"Z{way}4{0 if way == 'R' else 1}")
        names.append(f"S{way}1{0 if way == 'R' else 1}")
        for step in (2, 3, 4):
            names += [f"S{way}{step}{r}" for r in (0, 1)]
    for j in range(4):
        names += [f"ST{j}{m}" for m in (1, 2, 3)]
    names += ["DQ1", "DQ2", "DQ3", "SY"]
    return {name: index for index, name in enumerate(names)}


MSG = message_table()


class Part:
    def __init__(self, ref, index=None):
        self.ref, self.index = ref, index

    def make(self):
        return self.ref if self.index is None else self.ref.at[self.index]

    @property
    def at(self):
        return Maker(self.ref)

    def __getitem__(self, index):
        return self.make()[index]

    def __setitem__(self, index, value):
        self.make()[index] = value


class Maker:
    def __init__(self, ref):
        self.ref = ref

    def __getitem__(self, index):
        return Part(self.ref, index)


def rel_of(j):
    return j + (j // 2) * (5 - 2 * j)


def body(
    heads_axis, q_ref, k_ref, v_ref, g_ref, qg_ref, kg_ref, cos_ref, sin_ref, p_ref, swap_ref,
    dq_ref, dk_ref, dv_ref, gain_ref,
    kv, qc, gc, e_a, g_a, e_b, g_b, e_d, g_d, sums, stbuf, stats, dqacc, dkd, dvd, dkacc, dvacc,
    dkv, ring, dqs, dqr, ysend, yrecv, gbuf, gsum,
    ssem, rsem, gssem, grsem,
):
    kv, qc, gc, stbuf, dkv, ring, dqs, dqr, ysend, yrecv = (
        Part(ref) for ref in (kv, qc, gc, stbuf, dkv, ring, dqs, dqr, ysend, yrecv)
    )
    ctx = lax.axis_index("ctx")
    head = lax.axis_index("head")
    z, x, y = ctx // (X * Y), (ctx // Y) % X, ctx % Y
    w = ctx % (X * Y)
    ys = (y, 1 - y)

    zpos = [lax.rem(z + off, Z) for off in range(Z)]
    xpos = [lax.rem(x + off, X) for off in range(X)]

    def zm(off):
        return zpos[off % Z]

    def xm(off):
        return xpos[off % X]

    def dev(zz, xx, yy):
        return ((zz * X + xx) * Y + yy, head)

    groups = (
        (z, Z, lambda j: (lax.rem(z + j, Z) * (X * Y) + w, head)),
        (w, X * Y, lambda j: (z * (X * Y) + lax.rem(w + j, X * Y), head)),
        (head, heads_axis, lambda j: (ctx, lax.rem(head + j, heads_axis))),
    )
    all_peers = [peer(j) for _, size, peer in groups for j in range(1, size)]

    barrier = pltpu.get_barrier_semaphore()
    for peer in all_peers:
        pl.semaphore_signal(barrier, inc=1, device_id=peer, device_id_type=pl.DeviceIdType.MESH)

    started = []

    def copy(name, src, dst, to):
        i = MSG[name]
        return pltpu.make_async_remote_copy(
            src_ref=src.make(), dst_ref=dst.make(), send_sem=ssem.at[i], recv_sem=rsem.at[i],
            device_id=to, device_id_type=pl.DeviceIdType.MESH,
        )

    def send(name, src, dst, to):
        copy(name, src, dst, to).start()
        started.append((name, src, dst, to))

    def arrived(name, dst):
        copy(name, dst, dst, (ctx, head)).wait_recv()

    xdev = [dev(z, xpos[m], y) for m in range(X)]
    right_x, left_x = dev(z, xm(1), y), dev(z, xm(-1), y)
    partner = dev(z, x, ys[1])
    side = {"R": (dev(zm(1), x, y), -1), "L": (dev(zm(-1), x, y), 1)}
    last = {"R": 0, "L": 1}

    swapped = swap_ref[0:1, :] > 0.5
    p_me = p_ref[...]
    p_rows = jnp.concatenate([p_me, p_me], axis=0).astype(BF16)

    def halves(v):
        first, second = v[:HALF], v[HALF:]
        return jnp.where(swapped, second, first), jnp.where(swapped, first, second)

    def rope(v):
        return v * cos_ref[...] + pltpu.roll(v, HALF, 1) * sin_ref[...]

    def unrope(v):
        return v * cos_ref[...] - pltpu.roll(v, HALF, 1) * sin_ref[...]

    def normed(v):
        inverse = lax.rsqrt(jnp.mean(v * v, axis=-1, keepdims=True) + EPS)
        return v * inverse, inverse

    kn, _ = normed(k_ref[...].astype(F32))
    k_lo, k_hi = halves(rope(kn * kg_ref[...]))
    v_lo, v_hi = halves(v_ref[...].astype(F32))
    kv[z, y, 0:HALF] = k_lo.astype(BF16)
    kv[z, y, HALF:D] = k_hi.astype(BF16)
    kv[z, y, D:KROWS] = p_rows
    kv[z, y, KROWS:KROWS + HALF] = v_lo.astype(BF16)
    kv[z, y, KROWS + HALF:KROWS + D] = v_hi.astype(BF16)
    for h in range(HEADS):
        rows = slice(h * HALF, (h + 1) * HALF)
        lo, hi = halves(g_ref[:, h * D:(h + 1) * D].astype(F32))
        gc[x, rows, 0:D] = lo.astype(BF16)
        gc[x, rows, D:] = hi.astype(BF16)

    pl.semaphore_wait(barrier, len(all_peers))

    send("Y", kv.at[z, y], kv.at[z, y], partner)
    send("GL", gc.at[x], gc.at[x], left_x)
    send("GR", gc.at[x], gc.at[x], right_x)
    for way in "RL":
        send(f"Z{way}10", kv.at[z, y], kv.at[z, y], side[way][0])

    for h in range(HEADS):
        rows = slice(h * HALF, (h + 1) * HALF)
        qn, _ = normed(q_ref[:, h * D:(h + 1) * D].astype(F32))
        lo, hi = halves(rope(qn * qg_ref[...]))
        qc[x, rows, 0:D] = lo.astype(BF16)
        qc[x, rows, D:] = hi.astype(BF16)
    qc[x, Q:, 0:D] = p_rows
    qc[x, Q:, D:] = p_rows
    send("QR", qc.at[x], qc.at[x], right_x)
    send("QL", qc.at[x], qc.at[x], left_x)

    zero = jnp.zeros((HALF, D), BF16)

    def diagonal(lo, hi):
        return jnp.concatenate(
            [jnp.concatenate([lo, zero], axis=1), jnp.concatenate([zero, hi], axis=1)], axis=0
        )

    def own_k():
        return diagonal(kv[z, y, 0:HALF], kv[z, y, HALF:D])

    scores = dot(own_k(), qc[x, 0:Q], NT)
    key_row = lax.broadcasted_iota(jnp.int32, (D, Q), 0) % HALF
    query_lane = lax.broadcasted_iota(jnp.int32, (D, Q), 1) % HALF
    exps = jnp.where(key_row <= query_lane, jnp.exp2(scores * (SCALE * LOG2E)), 0.0)
    own_v = diagonal(kv[z, y, KROWS:KROWS + HALF], kv[z, y, KROWS + HALF:KROWS + D])
    probs_grad = dot(own_v, gc[x], NT)
    e_d[...] = exps
    g_d[...] = probs_grad
    both = exps * probs_grad
    for part in range(2):
        rows = slice(part * HALF, (part + 1) * HALF)
        sums[part] = exps[rows].reshape(8, 8, Q).sum(0)
        sums[2 + part] = both[rows].reshape(8, 8, Q).sum(0)

    arrived("Y", kv.at[z, ys[1]])
    for way in "RL":
        send(f"Z{way}11", kv.at[z, ys[1]], kv.at[z, ys[1]], side[way][0])

    def kv_progress(d):
        for r in (0, 1):
            for way in "RL":
                to, sign = side[way]
                if d == 4 and r != last[way]:
                    continue
                block = kv.at[zm(sign * d), ys[r]]
                arrived(f"Z{way}{d}{r}", block)
                if d < 3 or (d == 3 and r == last[way]):
                    send(f"Z{way}{d + 1}{r}", block, block, to)

    def block_rows(k, first, count):
        near = lax.rem(z + k, Z)
        far = lax.rem(z + (Z - 1) - k, Z)
        return jnp.concatenate(
            [kv[near, :, first:first + count, :], kv[far, :, first:first + count, :]], axis=0
        )

    def block_masks(k, b):
        pj = block_rows(k, D, 16).astype(F32)[:, 0:8, :]
        pq = qc[b, Q:, 0:D].astype(F32)[None, 0:8]
        early = jnp.where(pj < pq, 1.0, 0.0)
        other = jnp.where(pj == pq, 0.0, 1.0)
        return early, other

    def wide(v):
        return jnp.concatenate([v, v, v, v], axis=-1)

    def joined(lo, hi, early):
        e = early[:, 0:1, :].astype(BF16)
        return jnp.concatenate([lo * e, hi * (1.0 - e).astype(BF16)], axis=-1).reshape(4 * HALF, 2 * D)

    def pass_one(k, b, u):
        early, other = block_masks(k, b)
        klo, khi = block_rows(k, 0, HALF), block_rows(k, HALF, HALF)
        vlo, vhi = block_rows(k, KROWS, HALF), block_rows(k, KROWS + HALF, HALF)
        ex = jnp.exp2(dot(klo.reshape(4 * HALF, D), qc[b, 0:Q, D:], NT) * (SCALE * LOG2E))
        gp = dot(vlo.reshape(4 * HALF, D), gc[b, :, D:], NT)
        e_a[u] = ex
        g_a[u] = gp
        sums[1] += ex.reshape(32, 8, Q).sum(0)
        sums[3] += (ex * gp).reshape(32, 8, Q).sum(0)
        ex = jnp.exp2(dot(joined(klo, khi, early), qc[b, 0:Q], NT) * (SCALE * LOG2E))
        ex = ex.reshape(4, HALF, Q) * wide(other[:, 0:1, :])
        gp = dot(joined(vlo, vhi, early), gc[b], NT).reshape(4, HALF, Q)
        e_b[u] = ex.reshape(4 * HALF, Q)
        g_b[u] = gp.reshape(4 * HALF, Q)
        part = ex.reshape(4, 8, 8, Q).sum(1)
        partg = (ex * gp).reshape(4, 8, 8, Q).sum(1)
        ew = wide(early)
        sums[0] += (part * ew).sum(0)
        sums[1] += (part * (1.0 - ew)).sum(0)
        sums[2] += (partg * ew).sum(0)
        sums[3] += (partg * (1.0 - ew)).sum(0)

    def query_progress(j, k):
        if j == 0:
            kv_progress(k + 1)
            if k == 3:
                arrived("GL", gc.at[xm(1)])
                send("G2", gc.at[xm(1)], gc.at[xm(1)], left_x)
                arrived("QR", qc.at[xm(-1)])
                send("Q2", qc.at[xm(-1)], qc.at[xm(-1)], right_x)
        if k == 0:
            if j == 1:
                arrived("QL", qc.at[xm(1)])
            elif j == 2:
                arrived("GR", gc.at[xm(-1)])
            elif j == 3:
                arrived("Q2", qc.at[xm(2)])
                arrived("G2", gc.at[xm(2)])

    def statistics_out(j):
        b = xm(rel_of(j))
        slot = stbuf.at[b, x]
        slot[...] = jnp.concatenate(
            [jnp.sum(sums[...], axis=1), jnp.zeros((4, Q), F32)], axis=0
        )
        for m in (1, 2, 3):
            send(f"ST{j}{m}", slot, slot, xdev[m])
        sums[...] = jnp.zeros((4, 8, Q), F32)

    def first_loop(i, carry):
        j, k = i // 4, i % 4
        for case in range(16):
            @pl.when(i == case)
            def _(case=case):
                query_progress(case // 4, case % 4)
        rel = rel_of(j)
        pass_one(k, lax.rem(x + rel, X), k * 4 + rel)
        for case in range(4):
            @pl.when(i == 4 * case + 3)
            def _(case=case):
                statistics_out(case)
        return carry

    lax.fori_loop(0, 16, first_loop, 0)

    for j in range(4):
        for m in (1, 2, 3):
            arrived(f"ST{j}{m}", stbuf.at[xm(rel_of(j) - m), xm(-m)])
    for b in range(4):
        total = stbuf[b, 0]
        for s in range(1, 4):
            total = total + stbuf[b, s]
        inv = 1.0 / total[0:2]
        stats[b] = jnp.concatenate([inv, total[2:4] * inv, jnp.zeros((4, Q), F32)], axis=0)

    rowsel = lax.broadcasted_iota(jnp.int32, (D, Q), 0) < HALF
    pr = e_d[...] * jnp.where(rowsel, stats[x, 0:1], stats[x, 1:2])
    gs = (pr * (g_d[...] - jnp.where(rowsel, stats[x, 2:3], stats[x, 3:4]))).astype(BF16)
    pr = pr.astype(BF16)
    top = lax.broadcasted_iota(jnp.int32, (D, D), 0) < HALF
    full = dot(pr, gc[x], NN)
    dvd[...] = jnp.where(top, full[:, 0:D], full[:, D:])
    full = dot(gs, qc[x, 0:Q], NN)
    dkd[...] = jnp.where(top, full[:, 0:D], full[:, D:]) * SCALE
    for m in (1, 2, 3):
        dqacc[m] = jnp.zeros((2 * D, Q), F32)
    dqacc[0] = dot(own_k(), gs, TN)

    def pass_two(k, b, rel, u):
        early, _ = block_masks(k, b)
        klo, khi = block_rows(k, 0, HALF), block_rows(k, HALF, HALF)
        pr = e_a[u] * stats[b, 1:2]
        gs = (pr * (g_a[u] - stats[b, 3:4])).astype(BF16)
        pr = pr.astype(BF16)
        dva = dot(pr, gc[b, :, D:], NN).reshape(4, HALF, D)
        dka = dot(gs, qc[b, 0:Q, D:], NN).reshape(4, HALF, D)
        dqacc[rel, D:, :] += dot(klo.reshape(4 * HALF, D), gs, TN)
        ew = wide(early[:, 0:1, :]) > 0.5
        invb = jnp.where(ew, stats[b, 0:1][None], stats[b, 1:2][None])
        delb = jnp.where(ew, stats[b, 2:3][None], stats[b, 3:4][None])
        pr = e_b[u].reshape(4, HALF, Q) * invb
        gs = (pr * (g_b[u].reshape(4, HALF, Q) - delb)).astype(BF16).reshape(4 * HALF, Q)
        pr = pr.astype(BF16).reshape(4 * HALF, Q)
        dvc = dot(pr, gc[b], NN).reshape(4, HALF, 2 * D)
        dkc = dot(gs, qc[b, 0:Q], NN).reshape(4, HALF, 2 * D)
        dqacc[rel] += dot(joined(klo, khi, early), gs, TN)
        e1 = early[:, 0:1, :]
        dkacc[:, 0:HALF] += dka + dkc[..., 0:D] * e1
        dkacc[:, HALF:] += dkc[..., D:] * (1.0 - e1)
        dvacc[:, 0:HALF] += dva + dvc[..., 0:D] * e1
        dvacc[:, HALF:] += dvc[..., D:] * (1.0 - e1)

    def clear():
        dkacc[...] = jnp.zeros((4, D, D), F32)
        dvacc[...] = jnp.zeros((4, D, D), F32)

    def reduce_step(k):
        for place, zz in enumerate((zm(k), zm(-k - 1))):
            rows = slice(2 * place, 2 * place + 2)
            dkv[zz, :, 0:D, :] = (dkacc[rows] * SCALE).astype(BF16)
            dkv[zz, :, D:, :] = dvacc[rows].astype(BF16)
        if k > 0:
            clear()
        if k == 3:
            for wi, way in enumerate("RL"):
                r = last[way]
                send(f"S{way}1{r}", dkv.at[zm(4), ys[r]], ring.at[wi, 0, r], side[way][0])
            return
        off = k + 1
        step = 4 - off
        for r in (0, 1):
            for wi, way in enumerate("RL"):
                zz = zm(off if way == "R" else -off)
                part = dkv.at[zz, ys[r]]
                if step > 1 or r == last[way]:
                    came = ring.at[wi, step - 1, r]
                    arrived(f"S{way}{step}{r}", came)
                    part[...] = (part[...].astype(F32) + came[...].astype(F32)).astype(BF16)
                send(f"S{way}{step + 1}{r}", part, ring.at[wi, step, r], side[way][0])

    clear()

    def second_loop(i, carry):
        k, j = 3 - i // 4, 3 - i % 4
        rel = rel_of(j)
        pass_two(k, lax.rem(x + rel, X), rel, k * 4 + rel)
        for case in range(12, 15):
            @pl.when(i == case)
            def _(case=case):
                m = rel_of(3 - case % 4)
                dqs[m - 1] = dqacc[m].astype(BF16)
                send(f"DQ{m}", dqs.at[m - 1], dqr.at[m - 1], xdev[m])
        for case in range(4):
            @pl.when(i == 4 * case + 3)
            def _(case=case):
                reduce_step(3 - case)
        return carry

    lax.fori_loop(0, 16, second_loop, 0)

    def own_sum(r):
        total = dkv[z, ys[r]].astype(F32)
        for wi in (0, 1):
            total = total + ring[wi, 3, r].astype(F32)
        return total

    for r in (1, 0):
        for way in "RL":
            wi = 0 if way == "R" else 1
            arrived(f"S{way}4{r}", ring.at[wi, 3, r])
        if r == 1:
            ysend[...] = own_sum(1).astype(BF16)
            send("SY", ysend, yrecv, partner)

    def stored(lo, hi):
        return jnp.concatenate(
            [jnp.where(swapped, hi, lo), jnp.where(swapped, lo, hi)], axis=0
        )

    def norm_back(g, xn, inverse, gain):
        s = g * gain
        return inverse * (s - xn * jnp.mean(s * xn, axis=-1, keepdims=True))

    whole = dqacc[0]
    for m in (1, 2, 3):
        arrived(f"DQ{m}", dqr.at[m - 1])
        whole = whole + dqr[m - 1].astype(F32)
    turned = jnp.transpose(whole) * SCALE
    gain_sum = jnp.zeros((1, D), F32)
    for h in range(HEADS):
        cols = slice(h * D, (h + 1) * D)
        rows = slice(h * HALF, (h + 1) * HALF)
        gq = unrope(stored(turned[rows, 0:D], turned[rows, D:]))
        qn, inverse = normed(q_ref[:, cols].astype(F32))
        gain_sum = gain_sum + jnp.sum(gq * qn, axis=0, keepdims=True)
        dq_ref[:, cols] = norm_back(gq, qn, inverse, qg_ref[...]).astype(BF16)

    arrived("SY", yrecv)
    own = own_sum(0) + yrecv[...].astype(F32)
    dk_own = own[0:D] + dkd[...]
    gk = unrope(stored(dk_own[:HALF], dk_own[HALF:]))
    kn, inverse = normed(k_ref[...].astype(F32))
    key_gain = jnp.sum(gk * kn, axis=0, keepdims=True)

    mine = jnp.concatenate([gain_sum, key_gain, jnp.zeros((6, D), F32)], axis=0)
    for stage, (me, size, peer) in enumerate(groups):
        gsum[stage] = mine
        gbuf[stage, me] = mine
        copies = []
        for j in range(1, size):
            c = pltpu.make_async_remote_copy(
                src_ref=gsum.at[stage], dst_ref=gbuf.at[stage, me],
                send_sem=gssem.at[stage, j], recv_sem=grsem.at[stage, j],
                device_id=peer(j), device_id_type=pl.DeviceIdType.MESH,
            )
            c.start()
            copies.append(c)
        if stage == 0:
            dk_ref[...] = norm_back(gk, kn, inverse, kg_ref[...]).astype(BF16)
            dv_own = own[D:] + dvd[...]
            dv_ref[...] = stored(dv_own[:HALF], dv_own[HALF:]).astype(BF16)
        for c in copies:
            c.wait()
        mine = gbuf[stage, 0]
        for j in range(1, size):
            mine = mine + gbuf[stage, j]
    gain_ref[...] = mine

    for name, src, dst, to in started:
        copy(name, src, dst, to).wait_send()


def shards(heads_axis, query_raw, key_before_norm, values, grads, q_gain, k_gain, tok_pos):
    first, second = tok_pos[0], tok_pos[HALF]
    run = (jnp.minimum(first, second) // HALF).astype(F32)
    p = jnp.full((8, D), run, F32)
    swap = jnp.full((8, D), (first > second).astype(F32), F32)
    frequency = jnp.power(F32(BASE), -(jnp.arange(HALF, dtype=F32) * (2.0 / D)))
    angles = tok_pos.astype(F32)[:, None] * frequency[None, :]
    cosine, sine = jnp.cos(angles), jnp.sin(angles)
    cos2 = jnp.concatenate([cosine, cosine], axis=-1)
    sin2 = jnp.concatenate([-sine, sine], axis=-1)
    vmem = pl.BlockSpec(memory_space=pltpu.VMEM)
    count = len(MSG)
    dq, dk, dv, gains = pl.pallas_call(
        functools.partial(body, heads_axis),
        out_shape=(
            jax.ShapeDtypeStruct((D, HEADS * D), BF16),
            jax.ShapeDtypeStruct((D, D), BF16),
            jax.ShapeDtypeStruct((D, D), BF16),
            jax.ShapeDtypeStruct((8, D), F32),
        ),
        in_specs=[vmem] * 10,
        out_specs=(vmem,) * 4,
        scratch_shapes=[
            pltpu.VMEM((Z, Y, KROWS + D, D), BF16),
            pltpu.VMEM((X, Q + 16, 2 * D), BF16),
            pltpu.VMEM((X, Q, 2 * D), BF16),
            pltpu.VMEM((16, 4 * HALF, Q), F32),
            pltpu.VMEM((16, 4 * HALF, Q), F32),
            pltpu.VMEM((16, 4 * HALF, Q), F32),
            pltpu.VMEM((16, 4 * HALF, Q), F32),
            pltpu.VMEM((D, Q), F32),
            pltpu.VMEM((D, Q), F32),
            pltpu.VMEM((4, 8, Q), F32),
            pltpu.VMEM((X, X, 8, Q), F32),
            pltpu.VMEM((X, 8, Q), F32),
            pltpu.VMEM((X, 2 * D, Q), F32),
            pltpu.VMEM((D, D), F32),
            pltpu.VMEM((D, D), F32),
            pltpu.VMEM((4, D, D), F32),
            pltpu.VMEM((4, D, D), F32),
            pltpu.VMEM((Z, Y, 2 * D, D), BF16),
            pltpu.VMEM((2, 4, 2, 2 * D, D), BF16),
            pltpu.VMEM((3, 2 * D, Q), BF16),
            pltpu.VMEM((3, 2 * D, Q), BF16),
            pltpu.VMEM((2 * D, D), BF16),
            pltpu.VMEM((2 * D, D), BF16),
            pltpu.VMEM((3, 8, 8, D), F32),
            pltpu.VMEM((3, 8, D), F32),
            pltpu.SemaphoreType.DMA((count,)),
            pltpu.SemaphoreType.DMA((count,)),
            pltpu.SemaphoreType.DMA((3, 8)),
            pltpu.SemaphoreType.DMA((3, 8)),
        ],
        compiler_params=pltpu.CompilerParams(
            collective_id=0, has_side_effects=True, vmem_limit_bytes=60 * 1024 * 1024
        ),
    )(
        query_raw, key_before_norm, values, grads,
        q_gain.reshape(1, D), k_gain.reshape(1, D), cos2, sin2, p, swap,
    )
    return dq, dk, dv, gains[0], gains[1]


def solution(mesh):
    split = P("ctx", "head")
    return jax.shard_map(
        functools.partial(shards, mesh.shape["head"]),
        mesh=mesh,
        in_specs=(split, split, split, split, P(), P(), P("ctx")),
        out_specs=(split, split, split, P(), P()),
        check_vma=False,
    )
```

time: 134 us -> 103 us (0.77)
  Pallas kernels: 123 us -> 91.8 us
    pallas_call x1, Pallas kernels: 123 us -> 91.8 us  [shards(): pl.pallas_call(functools.partial(body, heads_axis), out_shape=(jax.ShapeD...]
where the time goes in v2:
time: 103 us
  Pallas kernels  91.8 us (89%)
  local copies, waits for them, and re-layouts  6.76 us (7%)
  between operations  3.28 us (3%)
  other arithmetic  1.07 us (1%)
    pallas_call x1, Pallas kernels, shards(): pl.pallas_call(functools.partial(body, heads_axis), out_shape=(jax.ShapeD...  91.8 us
    unnamed x9, local copies, waits for them, and re-layouts  3.71 us

profile of v2, /device:TPU:1, one launch (start us, length us, event | category | flops | bytes accessed | tf_op | source)
XLA Modules:
  0.0 102.9 jit_solution(6399861935027857156)
XLA Ops:
  0.6 0.0 copy-start.2
  0.6 0.6 copy-done.2
  1.3 0.6 fusion.1
  4.5 0.6 broadcast_in_dim.8.p_ref
  5.1 0.6 broadcast_in_dim.9.swap_ref
  5.7 0.3 fusion
  6.0 0.7 pad_maximum_fusion
  6.8 91.8 %shard_map.110 = (bf16[128,1024]{1,0:T(8,128)(2,1)}, bf16[128,128]{1,0:T(8,128)(2,1)}, bf16[128,128]{1,0:T(8,128)(2,1)}, f32[8,128]{1,0:T(8,128)}) custom-call(bf16[128,1024]{1,0:T(8,128)(2,1)} %q_ref.1, bf16[128,128]{1,0:T(8,128)(2,1)} %k_ref.1, bf16[128,128]{1,0:T(8,128)(2,1)} %v_ref.1, bf16[128,1024]{1,0:T(8,128)(2,1)} %g_ref.1, f32[1,128]{1,0:T(1,128)} %bitcast.8, ...), custom_call_target="tpu_custom_call" | custom-call | tf_op jit(solution)/shard_map/pallas_call | solution.py:495
  98.5 1.3 %slice_bitcast_fusion = (f32[128]{0:T(128)}, f32[128]{0:T(128)}) fusion(f32[8,128]{1,0:T(8,128)} %get-tuple-element.12), kind=kLoop, calls=%fused_computation.5 | loop fusion | bytes 2048 | tf_op jit(solution)/shard_map/squeeze | solution.py:543
  99.8 0.0 copy-start.1
  99.8 1.7 %copy.15 = bf16[128,1024]{1,0:T(8,128)(2,1)} copy(bf16[128,1024]{1,0:T(8,128)(2,1)} %get-tuple-element.27) | data formatting | bytes 524288
  101.5 0.0 copy-done.1
  101.5 0.0 copy-start
  101.5 0.6 copy.16
  102.1 0.2 copy-done
  102.3 0.6 copy.17
  (2 shorter events, 0.0 us)
Async XLA Ops:
  0.6 0.7 copy-start.2
  99.8 1.7 %copy-start.1 = (bf16[128,128]{1,0:T(8,128)(2,1)S(1)}, bf16[128,128]{1,0:T(8,128)(2,1)}, u32[]{:S(2)}) copy-start(bf16[128,128]{1,0:T(8,128)(2,1)} %get-tuple-element.28) | copy-start | bytes 98308
  101.5 0.8 copy-start

commit v3 on v2

--- a/solution.py
+++ b/solution.py
@@ -2,6 +2,7 @@
 
 import jax
 import jax.numpy as jnp
+import numpy as np
 from jax import lax
 from jax.experimental import pallas as pl
 from jax.experimental.pallas import tpu as pltpu
@@ -76,9 +77,9 @@
 
 
 def body(
-    heads_axis, q_ref, k_ref, v_ref, g_ref, qg_ref, kg_ref, cos_ref, sin_ref, p_ref, swap_ref,
+    heads_axis, q_ref, k_ref, v_ref, g_ref, qg_ref, kg_ref, pos_ref, freq_ref,
     dq_ref, dk_ref, dv_ref, gain_ref,
-    kv, qc, gc, e_a, g_a, e_b, g_b, e_d, g_d, sums, stbuf, stats, dqacc, dkd, dvd, dkacc, dvacc,
+    cos_ref, sin_ref, kv, qc, gc, e_a, g_a, e_b, g_b, e_d, g_d, sums, stbuf, stats, dqacc, dkd, dvd, dkacc, dvacc,
     dkv, ring, dqs, dqr, ysend, yrecv, gbuf, gsum,
     ssem, rsem, gssem, grsem,
 ):
@@ -136,8 +137,13 @@
     side = {"R": (dev(zm(1), x, y), -1), "L": (dev(zm(-1), x, y), 1)}
     last = {"R": 0, "L": 1}
 
-    swapped = swap_ref[0:1, :] > 0.5
-    p_me = p_ref[...]
+    positions = jnp.broadcast_to(pos_ref[...].astype(F32), (8, D))
+    in_first = lax.broadcasted_iota(jnp.int32, (8, D), 1) < HALF
+    first_top = jnp.max(jnp.where(in_first, positions, -1.0), axis=1, keepdims=True)
+    second_top = jnp.max(jnp.where(in_first, -1.0, positions), axis=1, keepdims=True)
+    swapped = jnp.broadcast_to(first_top > second_top, (8, D))[0:1]
+    lowest = jnp.min(positions, axis=1, keepdims=True)
+    p_me = jnp.broadcast_to(jnp.floor(lowest * (1.0 / HALF)), (8, D))
     p_rows = jnp.concatenate([p_me, p_me], axis=0).astype(BF16)
 
     def halves(v):
@@ -153,6 +159,22 @@
     def normed(v):
         inverse = lax.rsqrt(jnp.mean(v * v, axis=-1, keepdims=True) + EPS)
         return v * inverse, inverse
+
+    for h in range(HEADS):
+        rows = slice(h * HALF, (h + 1) * HALF)
+        lo, hi = halves(g_ref[:, h * D:(h + 1) * D].astype(F32))
+        gc[x, rows, 0:D] = lo.astype(BF16)
+        gc[x, rows, D:] = hi.astype(BF16)
+
+    pl.semaphore_wait(barrier, len(all_peers))
+
+    send("GL", gc.at[x], gc.at[x], left_x)
+    send("GR", gc.at[x], gc.at[x], right_x)
+
+    angles = jnp.transpose(jnp.broadcast_to(positions[0:1], (D, D))) * freq_ref[...]
+    cos_ref[...] = jnp.cos(angles)
+    turn = jnp.sin(angles)
+    sin_ref[...] = jnp.where(lax.broadcasted_iota(jnp.int32, (D, D), 1) < HALF, -turn, turn)
 
     kn, _ = normed(k_ref[...].astype(F32))
     k_lo, k_hi = halves(rope(kn * kg_ref[...]))
@@ -162,17 +184,7 @@
     kv[z, y, D:KROWS] = p_rows
     kv[z, y, KROWS:KROWS + HALF] = v_lo.astype(BF16)
     kv[z, y, KROWS + HALF:KROWS + D] = v_hi.astype(BF16)
-    for h in range(HEADS):
-        rows = slice(h * HALF, (h + 1) * HALF)
-        lo, hi = halves(g_ref[:, h * D:(h + 1) * D].astype(F32))
-        gc[x, rows, 0:D] = lo.astype(BF16)
-        gc[x, rows, D:] = hi.astype(BF16)
-
-    pl.semaphore_wait(barrier, len(all_peers))
-
     send("Y", kv.at[z, y], kv.at[z, y], partner)
-    send("GL", gc.at[x], gc.at[x], left_x)
-    send("GR", gc.at[x], gc.at[x], right_x)
     for way in "RL":
         send(f"Z{way}10", kv.at[z, y], kv.at[z, y], side[way][0])
 
@@ -206,25 +218,55 @@
     e_d[...] = exps
     g_d[...] = probs_grad
     both = exps * probs_grad
+    for j in (1, 2, 3):
+        sums[j] = jnp.zeros((4, 8, Q), F32)
     for part in range(2):
         rows = slice(part * HALF, (part + 1) * HALF)
-        sums[part] = exps[rows].reshape(8, 8, Q).sum(0)
-        sums[2 + part] = both[rows].reshape(8, 8, Q).sum(0)
-
-    arrived("Y", kv.at[z, ys[1]])
-    for way in "RL":
-        send(f"Z{way}11", kv.at[z, ys[1]], kv.at[z, ys[1]], side[way][0])
-
-    def kv_progress(d):
-        for r in (0, 1):
-            for way in "RL":
-                to, sign = side[way]
-                if d == 4 and r != last[way]:
-                    continue
-                block = kv.at[zm(sign * d), ys[r]]
-                arrived(f"Z{way}{d}{r}", block)
-                if d < 3 or (d == 3 and r == last[way]):
-                    send(f"Z{way}{d + 1}{r}", block, block, to)
+        sums[0, part] = exps[rows].reshape(8, 8, Q).sum(0)
+        sums[0, 2 + part] = both[rows].reshape(8, 8, Q).sum(0)
+
+    def kv_progress(r, d):
+        for way in "RL":
+            to, sign = side[way]
+            if d == 4 and r != last[way]:
+                continue
+            block = kv.at[zm(sign * d), ys[r]]
+            arrived(f"Z{way}{d}{r}", block)
+            if d < 3 or (d == 3 and r == last[way]):
+                send(f"Z{way}{d + 1}{r}", block, block, to)
+
+    def y_progress():
+        arrived("Y", kv.at[z, ys[1]])
+        for way in "RL":
+            send(f"Z{way}11", kv.at[z, ys[1]], kv.at[z, ys[1]], side[way][0])
+
+    def gradient_forward():
+        arrived("GL", gc.at[xm(1)])
+        send("G2", gc.at[xm(1)], gc.at[xm(1)], left_x)
+
+    def query_forward():
+        arrived("QR", qc.at[xm(-1)])
+        send("Q2", qc.at[xm(-1)], qc.at[xm(-1)], right_x)
+
+    def far_queries():
+        arrived("Q2", qc.at[xm(2)])
+        arrived("G2", gc.at[xm(2)])
+
+    def key_event(r, d):
+        return lambda: kv_progress(r, d)
+
+    events = {
+        0: (key_event(0, 1), y_progress, key_event(0, 2), gradient_forward, key_event(1, 1)),
+        1: (
+            key_event(0, 3), key_event(1, 2), query_forward,
+            lambda: arrived("QL", qc.at[xm(1)]),
+        ),
+        2: (lambda: arrived("GR", gc.at[xm(-1)]),),
+        3: (key_event(0, 4),),
+        6: (key_event(1, 3),),
+        9: (key_event(1, 4),),
+        12: (far_queries,),
+    }
 
     def block_rows(k, first, count):
         near = lax.rem(z + k, Z)
@@ -247,7 +289,7 @@
         e = early[:, 0:1, :].astype(BF16)
         return jnp.concatenate([lo * e, hi * (1.0 - e).astype(BF16)], axis=-1).reshape(4 * HALF, 2 * D)
 
-    def pass_one(k, b, u):
+    def pass_one(k, j, b, u):
         early, other = block_masks(k, b)
         klo, khi = block_rows(k, 0, HALF), block_rows(k, HALF, HALF)
         vlo, vhi = block_rows(k, KROWS, HALF), block_rows(k, KROWS + HALF, HALF)
@@ -255,8 +297,8 @@
         gp = dot(vlo.reshape(4 * HALF, D), gc[b, :, D:], NT)
         e_a[u] = ex
         g_a[u] = gp
-        sums[1] += ex.reshape(32, 8, Q).sum(0)
-        sums[3] += (ex * gp).reshape(32, 8, Q).sum(0)
+        sums[j, 1] += ex.reshape(32, 8, Q).sum(0)
+        sums[j, 3] += (ex * gp).reshape(32, 8, Q).sum(0)
         ex = jnp.exp2(dot(joined(klo, khi, early), qc[b, 0:Q], NT) * (SCALE * LOG2E))
         ex = ex.reshape(4, HALF, Q) * wide(other[:, 0:1, :])
         gp = dot(joined(vlo, vhi, early), gc[b], NT).reshape(4, HALF, Q)
@@ -265,50 +307,35 @@
         part = ex.reshape(4, 8, 8, Q).sum(1)
         partg = (ex * gp).reshape(4, 8, 8, Q).sum(1)
         ew = wide(early)
-        sums[0] += (part * ew).sum(0)
-        sums[1] += (part * (1.0 - ew)).sum(0)
-        sums[2] += (partg * ew).sum(0)
-        sums[3] += (partg * (1.0 - ew)).sum(0)
-
-    def query_progress(j, k):
-        if j == 0:
-            kv_progress(k + 1)
-            if k == 3:
-                arrived("GL", gc.at[xm(1)])
-                send("G2", gc.at[xm(1)], gc.at[xm(1)], left_x)
-                arrived("QR", qc.at[xm(-1)])
-                send("Q2", qc.at[xm(-1)], qc.at[xm(-1)], right_x)
-        if k == 0:
-            if j == 1:
-                arrived("QL", qc.at[xm(1)])
-            elif j == 2:
-                arrived("GR", gc.at[xm(-1)])
-            elif j == 3:
-                arrived("Q2", qc.at[xm(2)])
-                arrived("G2", gc.at[xm(2)])
+        sums[j, 0] += (part * ew).sum(0)
+        sums[j, 1] += (part * (1.0 - ew)).sum(0)
+        sums[j, 2] += (partg * ew).sum(0)
+        sums[j, 3] += (partg * (1.0 - ew)).sum(0)
 
     def statistics_out(j):
         b = xm(rel_of(j))
         slot = stbuf.at[b, x]
         slot[...] = jnp.concatenate(
-            [jnp.sum(sums[...], axis=1), jnp.zeros((4, Q), F32)], axis=0
+            [jnp.sum(sums[j], axis=1), jnp.zeros((4, Q), F32)], axis=0
         )
         for m in (1, 2, 3):
             send(f"ST{j}{m}", slot, slot, xdev[m])
-        sums[...] = jnp.zeros((4, 8, Q), F32)
 
     def first_loop(i, carry):
-        j, k = i // 4, i % 4
-        for case in range(16):
+        far = i // 12
+        k = (1 - far) * (i // 3) + far * (i - 12)
+        j = (1 - far) * (i % 3) + far * 3
+        for case, steps in events.items():
             @pl.when(i == case)
-            def _(case=case):
-                query_progress(case // 4, case % 4)
+            def _(steps=steps):
+                for step in steps:
+                    step()
         rel = rel_of(j)
-        pass_one(k, lax.rem(x + rel, X), k * 4 + rel)
-        for case in range(4):
-            @pl.when(i == 4 * case + 3)
-            def _(case=case):
-                statistics_out(case)
+        pass_one(k, j, lax.rem(x + rel, X), k * 4 + rel)
+        for case, done in ((9, 0), (10, 1), (11, 2), (15, 3)):
+            @pl.when(i == case)
+            def _(done=done):
+                statistics_out(done)
         return carry
 
     lax.fori_loop(0, 16, first_loop, 0)
@@ -334,6 +361,9 @@
     dkd[...] = jnp.where(top, full[:, 0:D], full[:, D:]) * SCALE
     for m in (1, 2, 3):
         dqacc[m] = jnp.zeros((2 * D, Q), F32)
+    for k in range(4):
+        dkacc[k] = jnp.zeros((4, D, D), F32)
+        dvacc[k] = jnp.zeros((4, D, D), F32)
     dqacc[0] = dot(own_k(), gs, TN)
 
     def pass_two(k, b, rel, u):
@@ -355,22 +385,16 @@
         dkc = dot(gs, qc[b, 0:Q], NN).reshape(4, HALF, 2 * D)
         dqacc[rel] += dot(joined(klo, khi, early), gs, TN)
         e1 = early[:, 0:1, :]
-        dkacc[:, 0:HALF] += dka + dkc[..., 0:D] * e1
-        dkacc[:, HALF:] += dkc[..., D:] * (1.0 - e1)
-        dvacc[:, 0:HALF] += dva + dvc[..., 0:D] * e1
-        dvacc[:, HALF:] += dvc[..., D:] * (1.0 - e1)
-
-    def clear():
-        dkacc[...] = jnp.zeros((4, D, D), F32)
-        dvacc[...] = jnp.zeros((4, D, D), F32)
+        dkacc[k, :, 0:HALF] += dka + dkc[..., 0:D] * e1
+        dkacc[k, :, HALF:] += dkc[..., D:] * (1.0 - e1)
+        dvacc[k, :, 0:HALF] += dva + dvc[..., 0:D] * e1
+        dvacc[k, :, HALF:] += dvc[..., D:] * (1.0 - e1)
 
     def reduce_step(k):
         for place, zz in enumerate((zm(k), zm(-k - 1))):
             rows = slice(2 * place, 2 * place + 2)
-            dkv[zz, :, 0:D, :] = (dkacc[rows] * SCALE).astype(BF16)
-            dkv[zz, :, D:, :] = dvacc[rows].astype(BF16)
-        if k > 0:
-            clear()
+            dkv[zz, :, 0:D, :] = (dkacc[k, rows] * SCALE).astype(BF16)
+            dkv[zz, :, D:, :] = dvacc[k, rows].astype(BF16)
         if k == 3:
             for wi, way in enumerate("RL"):
                 r = last[way]
@@ -388,20 +412,23 @@
                     part[...] = (part[...].astype(F32) + came[...].astype(F32)).astype(BF16)
                 send(f"S{way}{step + 1}{r}", part, ring.at[wi, step, r], side[way][0])
 
-    clear()
+
+    def queries_out(m):
+        dqs[m - 1] = dqacc[m].astype(BF16)
+        send(f"DQ{m}", dqs.at[m - 1], dqr.at[m - 1], xdev[m])
 
     def second_loop(i, carry):
-        k, j = 3 - i // 4, 3 - i % 4
+        near = (i + 12) // 16
+        k = (1 - near) * (3 - i) + near * (3 - (i + 8) // 3 + 4)
+        j = (1 - near) * 3 + near * (2 - (i + 8) % 3)
         rel = rel_of(j)
         pass_two(k, lax.rem(x + rel, X), rel, k * 4 + rel)
-        for case in range(12, 15):
+        for case, m in ((3, 2), (13, 3), (14, 1)):
             @pl.when(i == case)
-            def _(case=case):
-                m = rel_of(3 - case % 4)
-                dqs[m - 1] = dqacc[m].astype(BF16)
-                send(f"DQ{m}", dqs.at[m - 1], dqr.at[m - 1], xdev[m])
+            def _(m=m):
+                queries_out(m)
         for case in range(4):
-            @pl.when(i == 4 * case + 3)
+            @pl.when(i == 3 * case + 6)
             def _(case=case):
                 reduce_step(3 - case)
         return carry
@@ -481,15 +508,8 @@
 
 
 def shards(heads_axis, query_raw, key_before_norm, values, grads, q_gain, k_gain, tok_pos):
-    first, second = tok_pos[0], tok_pos[HALF]
-    run = (jnp.minimum(first, second) // HALF).astype(F32)
-    p = jnp.full((8, D), run, F32)
-    swap = jnp.full((8, D), (first > second).astype(F32), F32)
-    frequency = jnp.power(F32(BASE), -(jnp.arange(HALF, dtype=F32) * (2.0 / D)))
-    angles = tok_pos.astype(F32)[:, None] * frequency[None, :]
-    cosine, sine = jnp.cos(angles), jnp.sin(angles)
-    cos2 = jnp.concatenate([cosine, cosine], axis=-1)
-    sin2 = jnp.concatenate([-sine, sine], axis=-1)
+    frequency = np.power(np.float32(BASE), -(np.arange(HALF, dtype=np.float32) * np.float32(2.0 / D)))
+    frequency = jnp.asarray(np.tile(frequency.astype(np.float32), 2).reshape(1, D))
     vmem = pl.BlockSpec(memory_space=pltpu.VMEM)
     count = len(MSG)
     dq, dk, dv, gains = pl.pallas_call(
@@ -500,9 +520,11 @@
             jax.ShapeDtypeStruct((D, D), BF16),
             jax.ShapeDtypeStruct((8, D), F32),
         ),
-        in_specs=[vmem] * 10,
+        in_specs=[vmem] * 8,
         out_specs=(vmem,) * 4,
         scratch_shapes=[
+            pltpu.VMEM((D, D), F32),
+            pltpu.VMEM((D, D), F32),
             pltpu.VMEM((Z, Y, KROWS + D, D), BF16),
             pltpu.VMEM((X, Q + 16, 2 * D), BF16),
             pltpu.VMEM((X, Q, 2 * D), BF16),
@@ -512,14 +534,14 @@
             pltpu.VMEM((16, 4 * HALF, Q), F32),
             pltpu.VMEM((D, Q), F32),
             pltpu.VMEM((D, Q), F32),
-            pltpu.VMEM((4, 8, Q), F32),
+            pltpu.VMEM((4, 4, 8, Q), F32),
             pltpu.VMEM((X, X, 8, Q), F32),
             pltpu.VMEM((X, 8, Q), F32),
             pltpu.VMEM((X, 2 * D, Q), F32),
             pltpu.VMEM((D, D), F32),
             pltpu.VMEM((D, D), F32),
-            pltpu.VMEM((4, D, D), F32),
-            pltpu.VMEM((4, D, D), F32),
+            pltpu.VMEM((4, 4, D, D), F32),
+            pltpu.VMEM((4, 4, D, D), F32),
             pltpu.VMEM((Z, Y, 2 * D, D), BF16),
             pltpu.VMEM((2, 4, 2, 2 * D, D), BF16),
             pltpu.VMEM((3, 2 * D, Q), BF16),
@@ -538,7 +560,7 @@
         ),
     )(
         query_raw, key_before_norm, values, grads,
-        q_gain.reshape(1, D), k_gain.reshape(1, D), cos2, sin2, p, swap,
+        q_gain.reshape(1, D), k_gain.reshape(1, D), tok_pos.reshape(1, D), frequency,
     )
     return dq, dk, dv, gains[0], gains[1]
 

time: 103 us -> 94.6 us (0.918)
  between operations: 3.28 us -> 0.65 us
  local copies, waits for them, and re-layouts: 6.76 us -> 4.33 us
  Pallas kernels: 91.8 us -> 89.4 us
  other arithmetic: 1.07 us -> 0 us
    pallas_call x1, Pallas kernels: 91.8 us -> 89.4 us  [shards(): pl.pallas_call(functools.partial(body, heads_axis), out_shape=(jax.ShapeD...]
    broadcast_in_dim x2 -> x0, local copies, waits for them, and re-layouts: 1.19 us -> none  [the longest x1 0.6 us: shards(): p = jnp.full((8, D), run, F32)]
    unnamed x9 -> x7, local copies, waits for them, and re-layouts: 3.71 us -> 3.06 us
where the time goes in v3:
time: 94.6 us; the launch traced here: 94.3 us
  Pallas kernels  89.4 us (95%)
  local copies, waits for them, and re-layouts  4.33 us (5%)
    pallas_call x1, Pallas kernels, shards(): pl.pallas_call(functools.partial(body, heads_axis), out_shape=(jax.ShapeD...  89.4 us
    unnamed x7, local copies, waits for them, and re-layouts  3.06 us

profile of v3, /device:TPU:1, one launch (start us, length us, event | category | flops | bytes accessed | tf_op | source)
XLA Modules:
  0.0 94.3 jit_solution(2047164999175668711)
XLA Ops:
  0.6 89.4 %shard_map.119 = (bf16[128,1024]{1,0:T(8,128)(2,1)}, bf16[128,128]{1,0:T(8,128)(2,1)}, bf16[128,128]{1,0:T(8,128)(2,1)}, f32[8,128]{1,0:T(8,128)}) custom-call(bf16[128,1024]{1,0:T(8,128)(2,1)} %q_ref.1, bf16[128,128]{1,0:T(8,128)(2,1)} %k_ref.1, bf16[128,128]{1,0:T(8,128)(2,1)} %v_ref.1, bf16[128,1024]{1,0:T(8,128)(2,1)} %g_ref.1, f32[1,128]{1,0:T(1,128)} %bitcast.7, ...), custom_call_target="tpu_custom_call" | custom-call | tf_op jit(solution)/shard_map/pallas_call | solution.py:515
  90.0 1.3 %slice_bitcast_fusion = (f32[128]{0:T(128)}, f32[128]{0:T(128)}) fusion(f32[8,128]{1,0:T(8,128)} %get-tuple-element.12), kind=kLoop, calls=%fused_computation | loop fusion | bytes 2048 | tf_op jit(solution)/shard_map/squeeze | solution.py:565
  91.3 0.0 copy-start.1
  91.3 1.7 %copy.16 = bf16[128,1024]{1,0:T(8,128)(2,1)} copy(bf16[128,1024]{1,0:T(8,128)(2,1)} %get-tuple-element.20) | data formatting | bytes 524288
  93.0 0.0 copy-done.1
  93.0 0.0 copy-start
  93.0 0.6 copy.17
  93.6 0.2 copy-done
  93.7 0.6 copy.18
Async XLA Ops:
  91.3 1.7 %copy-start.1 = (bf16[128,128]{1,0:T(8,128)(2,1)S(1)}, bf16[128,128]{1,0:T(8,128)(2,1)}, u32[]{:S(2)}) copy-start(bf16[128,128]{1,0:T(8,128)(2,1)} %get-tuple-element.21) | copy-start | bytes 98308
  93.0 0.8 copy-start

commit v4 on v3

--- a/solution.py
+++ b/solution.py
@@ -79,7 +79,7 @@
 def body(
     heads_axis, q_ref, k_ref, v_ref, g_ref, qg_ref, kg_ref, pos_ref, freq_ref,
     dq_ref, dk_ref, dv_ref, gain_ref,
-    cos_ref, sin_ref, kv, qc, gc, e_a, g_a, e_b, g_b, e_d, g_d, sums, stbuf, stats, dqacc, dkd, dvd, dkacc, dvacc,
+    cos_ref, sin_ref, kv, qc, gc, e_a, g_a, e_b, g_b, e_d, g_d, sums, stbuf, stats, dqacc, dkacc, dvacc, ct_ref, st_ref, qcos, qsin, freq_col,
     dkv, ring, dqs, dqr, ysend, yrecv, gbuf, gsum,
     ssem, rsem, gssem, grsem,
 ):
@@ -340,6 +340,24 @@
 
     lax.fori_loop(0, 16, first_loop, 0)
 
+    token_row = (lax.broadcasted_iota(jnp.int32, (D, D), 0) % HALF).astype(F32)
+    twice = token_row * (2.0 * freq_ref[...])
+    ct_ref[...] = jnp.cos(twice)
+    st_ref[...] = jnp.sin(twice)
+    freq_col[...] = jnp.transpose(jnp.broadcast_to(freq_ref[...], (D, D)))[0:HALF]
+    token_lane = (lax.broadcasted_iota(jnp.int32, (HALF, D), 1) % HALF).astype(F32)
+
+    def query_tables(rel, carry):
+        early_run = jnp.max(qc[lax.rem(x + rel, X), Q:, 0:D].astype(F32), axis=0, keepdims=True)
+        for part in range(2):
+            run = early_run if part == 0 else (2 * X * Y * Z - 1) - early_run
+            angle = (run * HALF + token_lane) * (2.0 * freq_col[...])
+            qcos[rel, part] = jnp.cos(angle)
+            qsin[rel, part] = jnp.sin(angle)
+        return carry
+
+    lax.fori_loop(0, X, query_tables, 0)
+
     for j in range(4):
         for m in (1, 2, 3):
             arrived(f"ST{j}{m}", stbuf.at[xm(rel_of(j) - m), xm(-m)])
@@ -355,15 +373,15 @@
     gs = (pr * (g_d[...] - jnp.where(rowsel, stats[x, 2:3], stats[x, 3:4]))).astype(BF16)
     pr = pr.astype(BF16)
     top = lax.broadcasted_iota(jnp.int32, (D, D), 0) < HALF
-    full = dot(pr, gc[x], NN)
-    dvd[...] = jnp.where(top, full[:, 0:D], full[:, D:])
-    full = dot(gs, qc[x, 0:Q], NN)
-    dkd[...] = jnp.where(top, full[:, 0:D], full[:, D:]) * SCALE
-    for m in (1, 2, 3):
-        dqacc[m] = jnp.zeros((2 * D, Q), F32)
     for k in range(4):
         dkacc[k] = jnp.zeros((4, D, D), F32)
         dvacc[k] = jnp.zeros((4, D, D), F32)
+    full = dot(pr, gc[x], NN)
+    dvacc[0, y] = jnp.where(top, full[:, 0:D], full[:, D:])
+    full = dot(gs, qc[x, 0:Q], NN)
+    dkacc[0, y] = jnp.where(top, full[:, 0:D], full[:, D:])
+    for m in (1, 2, 3):
+        dqacc[m] = jnp.zeros((2 * D, Q), F32)
     dqacc[0] = dot(own_k(), gs, TN)
 
     def pass_two(k, b, rel, u):
@@ -392,6 +410,8 @@
 
     def reduce_step(k):
         for place, zz in enumerate((zm(k), zm(-k - 1))):
+            if zz is zpos[0]:
+                continue
             rows = slice(2 * place, 2 * place + 2)
             dkv[zz, :, 0:D, :] = (dkacc[k, rows] * SCALE).astype(BF16)
             dkv[zz, :, D:, :] = dvacc[k, rows].astype(BF16)
@@ -435,8 +455,99 @@
 
     lax.fori_loop(0, 16, second_loop, 0)
 
+    first_lanes = lax.broadcasted_iota(jnp.int32, (1, D), 1) < HALF
+
+    def key_share(k, carry):
+        plain, cosined, sined = carry
+        grad = dkacc[k].reshape(4 * D, D)
+        rot = block_rows(k, 0, D).astype(F32).reshape(4 * D, D)
+        straight = (grad * rot).reshape(4, 2, HALF, D)
+        crossed = (grad * pltpu.roll(rot, HALF, 1)).reshape(4, 2, HALF, D)
+        ct, st = ct_ref[0:HALF], st_ref[0:HALF]
+        early_run = block_rows(k, D, 16).astype(F32)[:, 0:1, :]
+        late_run = (2 * X * Y * Z - 1) - early_run
+        run = jnp.concatenate([early_run[:, None], late_run[:, None]], axis=1)
+        angle = run * (2.0 * HALF * freq_ref[...])
+        cp, sp = jnp.cos(angle), jnp.sin(angle)
+
+        def over_tokens(v):
+            return jnp.sum(v, axis=2, keepdims=True)
+
+        plain = plain + jnp.sum(over_tokens(straight), axis=(0, 1))
+        cosined = cosined + jnp.sum(
+            cp * over_tokens(straight * ct) - sp * over_tokens(straight * st), axis=(0, 1)
+        )
+        sined = sined + jnp.sum(
+            sp * over_tokens(crossed * ct) + cp * over_tokens(crossed * st), axis=(0, 1)
+        )
+        return plain, cosined, sined
+
+    none = jnp.zeros((1, D), F32)
+    plain, cosined, sined = lax.fori_loop(0, 4, key_share, (none, none, none))
+
+    def swap_lanes(v):
+        return pltpu.roll(jnp.broadcast_to(v, (8, D)), HALF, 1)[0:1]
+
+    both_sines = sined + swap_lanes(sined)
+    key_gain = plain + swap_lanes(plain) + cosined - swap_lanes(cosined)
+    key_gain = key_gain + jnp.where(first_lanes, both_sines, -both_sines)
+    key_gain = key_gain * (0.5 * SCALE) / kg_ref[...]
+
+    row_id = lax.broadcasted_iota(jnp.int32, (2 * D, 2 * D), 0)
+    lane_id = lax.broadcasted_iota(jnp.int32, (2 * D, 2 * D), 1)
+    identity = jnp.where(row_id == lane_id, 1.0, 0.0).astype(BF16)
+
+    def over_heads(v):
+        return v[:, 0:D] + v[:, D:2 * D] + v[:, 2 * D:3 * D] + v[:, 3 * D:]
+
+    def query_share(rel, carry):
+        plain, turned = carry
+        rot = dot(identity, qc[lax.rem(x + rel, X), 0:Q], NT)
+        grad = dqacc[rel]
+        for part in range(2):
+            a, b = grad[part * D:part * D + HALF], grad[part * D + HALF:part * D + D]
+            e, f = rot[part * D:part * D + HALF], rot[part * D + HALF:part * D + D]
+            ae, bf = over_heads(a * e), over_heads(b * f)
+            plain = plain + ae + bf
+            turned = turned + qcos[rel, part] * (ae - bf) + qsin[rel, part] * over_heads(a * f + b * e)
+        return plain, turned
+
+    none = jnp.zeros((HALF, D), F32)
+    plain, turned = lax.fori_loop(0, X, query_share, (none, none))
+    query_gain = jnp.transpose(jnp.concatenate([plain + turned, plain - turned], axis=0))
+    query_gain = jnp.sum(query_gain, axis=0, keepdims=True) * (0.5 * SCALE) / qg_ref[...]
+
+    def gain_copies(stage):
+        me, size, peer = groups[stage]
+        return [
+            pltpu.make_async_remote_copy(
+                src_ref=gsum.at[stage], dst_ref=gbuf.at[stage, me],
+                send_sem=gssem.at[stage, j], recv_sem=grsem.at[stage, j],
+                device_id=peer(j), device_id_type=pl.DeviceIdType.MESH,
+            )
+            for j in range(1, size)
+        ]
+
+    def gain_start(stage, mine):
+        gsum[stage] = mine
+        gbuf[stage, groups[stage][0]] = mine
+        copies = gain_copies(stage)
+        for c in copies:
+            c.start()
+        return copies
+
+    def gain_finish(stage, copies):
+        for c in copies:
+            c.wait()
+        total = gbuf[stage, 0]
+        for j in range(1, groups[stage][1]):
+            total = total + gbuf[stage, j]
+        return total
+
+    copies = gain_start(0, jnp.concatenate([query_gain, key_gain, jnp.zeros((6, D), F32)], axis=0))
+
     def own_sum(r):
-        total = dkv[z, ys[r]].astype(F32)
+        total = jnp.concatenate([dkacc[0, ys[r]] * SCALE, dvacc[0, ys[r]]], axis=0)
         for wi in (0, 1):
             total = total + ring[wi, 3, r].astype(F32)
         return total
@@ -449,6 +560,8 @@
             ysend[...] = own_sum(1).astype(BF16)
             send("SY", ysend, yrecv, partner)
 
+    copies = gain_start(1, gain_finish(0, copies))
+
     def stored(lo, hi):
         return jnp.concatenate(
             [jnp.where(swapped, hi, lo), jnp.where(swapped, lo, hi)], axis=0
@@ -463,45 +576,23 @@
         arrived(f"DQ{m}", dqr.at[m - 1])
         whole = whole + dqr[m - 1].astype(F32)
     turned = jnp.transpose(whole) * SCALE
-    gain_sum = jnp.zeros((1, D), F32)
     for h in range(HEADS):
         cols = slice(h * D, (h + 1) * D)
         rows = slice(h * HALF, (h + 1) * HALF)
         gq = unrope(stored(turned[rows, 0:D], turned[rows, D:]))
         qn, inverse = normed(q_ref[:, cols].astype(F32))
-        gain_sum = gain_sum + jnp.sum(gq * qn, axis=0, keepdims=True)
         dq_ref[:, cols] = norm_back(gq, qn, inverse, qg_ref[...]).astype(BF16)
+
+    copies = gain_start(2, gain_finish(1, copies))
 
     arrived("SY", yrecv)
     own = own_sum(0) + yrecv[...].astype(F32)
-    dk_own = own[0:D] + dkd[...]
-    gk = unrope(stored(dk_own[:HALF], dk_own[HALF:]))
+    gk = unrope(stored(own[:HALF], own[HALF:D]))
     kn, inverse = normed(k_ref[...].astype(F32))
-    key_gain = jnp.sum(gk * kn, axis=0, keepdims=True)
-
-    mine = jnp.concatenate([gain_sum, key_gain, jnp.zeros((6, D), F32)], axis=0)
-    for stage, (me, size, peer) in enumerate(groups):
-        gsum[stage] = mine
-        gbuf[stage, me] = mine
-        copies = []
-        for j in range(1, size):
-            c = pltpu.make_async_remote_copy(
-                src_ref=gsum.at[stage], dst_ref=gbuf.at[stage, me],
-                send_sem=gssem.at[stage, j], recv_sem=grsem.at[stage, j],
-                device_id=peer(j), device_id_type=pl.DeviceIdType.MESH,
-            )
-            c.start()
-            copies.append(c)
-        if stage == 0:
-            dk_ref[...] = norm_back(gk, kn, inverse, kg_ref[...]).astype(BF16)
-            dv_own = own[D:] + dvd[...]
-            dv_ref[...] = stored(dv_own[:HALF], dv_own[HALF:]).astype(BF16)
-        for c in copies:
-            c.wait()
-        mine = gbuf[stage, 0]
-        for j in range(1, size):
-            mine = mine + gbuf[stage, j]
-    gain_ref[...] = mine
+    dk_ref[...] = norm_back(gk, kn, inverse, kg_ref[...]).astype(BF16)
+    dv_ref[...] = stored(own[D:D + HALF], own[D + HALF:]).astype(BF16)
+
+    gain_ref[...] = gain_finish(2, copies)
 
     for name, src, dst, to in started:
         copy(name, src, dst, to).wait_send()
@@ -538,10 +629,13 @@
             pltpu.VMEM((X, X, 8, Q), F32),
             pltpu.VMEM((X, 8, Q), F32),
             pltpu.VMEM((X, 2 * D, Q), F32),
+            pltpu.VMEM((4, 4, D, D), F32),
+            pltpu.VMEM((4, 4, D, D), F32),
             pltpu.VMEM((D, D), F32),
             pltpu.VMEM((D, D), F32),
-            pltpu.VMEM((4, 4, D, D), F32),
-            pltpu.VMEM((4, 4, D, D), F32),
+            pltpu.VMEM((X, 2, HALF, D), F32),
+            pltpu.VMEM((X, 2, HALF, D), F32),
+            pltpu.VMEM((HALF, D), F32),
             pltpu.VMEM((Z, Y, 2 * D, D), BF16),
             pltpu.VMEM((2, 4, 2, 2 * D, D), BF16),
             pltpu.VMEM((3, 2 * D, Q), BF16),

time: 94.6 us -> 89.1 us (0.942)
  Pallas kernels: 89.4 us -> 83.9 us
    pallas_call x1, Pallas kernels: 89.4 us -> 83.9 us  [shards(): pl.pallas_call(functools.partial(body, heads_axis), out_shape=(jax.ShapeD...]
where the time goes in v4:
time: 89.1 us; the launch traced here: 88.9 us
  Pallas kernels  83.9 us (94%)
  local copies, waits for them, and re-layouts  4.33 us (5%)
    pallas_call x1, Pallas kernels, shards(): pl.pallas_call(functools.partial(body, heads_axis), out_shape=(jax.ShapeD...  83.9 us
    unnamed x7, local copies, waits for them, and re-layouts  3.06 us

profile of v4, /device:TPU:1, one launch (start us, length us, event | category | flops | bytes accessed | tf_op | source)
XLA Modules:
  0.0 88.9 jit_solution(1940851681011552707)
XLA Ops:
  0.6 83.9 %shard_map.119 = (bf16[128,1024]{1,0:T(8,128)(2,1)}, bf16[128,128]{1,0:T(8,128)(2,1)}, bf16[128,128]{1,0:T(8,128)(2,1)}, f32[8,128]{1,0:T(8,128)}) custom-call(bf16[128,1024]{1,0:T(8,128)(2,1)} %q_ref.1, bf16[128,128]{1,0:T(8,128)(2,1)} %k_ref.1, bf16[128,128]{1,0:T(8,128)(2,1)} %v_ref.1, bf16[128,1024]{1,0:T(8,128)(2,1)} %g_ref.1, f32[1,128]{1,0:T(1,128)} %bitcast.7, ...), custom_call_target="tpu_custom_call" | custom-call | tf_op jit(solution)/shard_map/pallas_call | solution.py:606
  84.5 1.3 %slice_bitcast_fusion = (f32[128]{0:T(128)}, f32[128]{0:T(128)}) fusion(f32[8,128]{1,0:T(8,128)} %get-tuple-element.12), kind=kLoop, calls=%fused_computation | loop fusion | bytes 2048 | tf_op jit(solution)/shard_map/squeeze | solution.py:659
  85.8 0.0 copy-start.1
  85.8 1.7 %copy.16 = bf16[128,1024]{1,0:T(8,128)(2,1)} copy(bf16[128,1024]{1,0:T(8,128)(2,1)} %get-tuple-element.20) | data formatting | bytes 524288
  87.5 0.0 copy-done.1
  87.5 0.0 copy-start
  87.5 0.6 copy.17
  88.1 0.2 copy-done
  88.3 0.6 copy.18
Async XLA Ops:
  85.8 1.7 %copy-start.1 = (bf16[128,128]{1,0:T(8,128)(2,1)S(1)}, bf16[128,128]{1,0:T(8,128)(2,1)}, u32[]{:S(2)}) copy-start(bf16[128,128]{1,0:T(8,128)(2,1)} %get-tuple-element.21) | copy-start | bytes 98308
  87.5 0.8 copy-start

commit v5 on v4

--- a/solution.py
+++ b/solution.py
@@ -29,11 +29,11 @@
 
 
 def message_table():
-    names = ["Y", "QR", "QL", "GR", "GL", "Q2", "G2"]
+    names = ["Y0", "Y1", "QR", "QL", "GR", "GL", "Q2", "G2"]
     for way in "RL":
         for step in (1, 2, 3):
-            names += [f"Z{way}{step}{r}" for r in (0, 1)]
-        names.append(f"Z{way}4{0 if way == 'R' else 1}")
+            names += [f"Z{way}{step}{r}{h}" for r in (0, 1) for h in (0, 1)]
+        names += [f"Z{way}4{0 if way == 'R' else 1}{h}" for h in (0, 1)]
         names.append(f"S{way}1{0 if way == 'R' else 1}")
         for step in (2, 3, 4):
             names += [f"S{way}{step}{r}" for r in (0, 1)]
@@ -78,7 +78,7 @@
 
 def body(
     heads_axis, q_ref, k_ref, v_ref, g_ref, qg_ref, kg_ref, pos_ref, freq_ref,
-    dq_ref, dk_ref, dv_ref, gain_ref,
+    dq_ref, dk_ref, dv_ref, qgain_ref, kgain_ref,
     cos_ref, sin_ref, kv, qc, gc, e_a, g_a, e_b, g_b, e_d, g_d, sums, stbuf, stats, dqacc, dkacc, dvacc, ct_ref, st_ref, qcos, qsin, freq_col,
     dkv, ring, dqs, dqr, ysend, yrecv, gbuf, gsum,
     ssem, rsem, gssem, grsem,
@@ -160,16 +160,6 @@
         inverse = lax.rsqrt(jnp.mean(v * v, axis=-1, keepdims=True) + EPS)
         return v * inverse, inverse
 
-    for h in range(HEADS):
-        rows = slice(h * HALF, (h + 1) * HALF)
-        lo, hi = halves(g_ref[:, h * D:(h + 1) * D].astype(F32))
-        gc[x, rows, 0:D] = lo.astype(BF16)
-        gc[x, rows, D:] = hi.astype(BF16)
-
-    pl.semaphore_wait(barrier, len(all_peers))
-
-    send("GL", gc.at[x], gc.at[x], left_x)
-    send("GR", gc.at[x], gc.at[x], right_x)
 
     angles = jnp.transpose(jnp.broadcast_to(positions[0:1], (D, D))) * freq_ref[...]
     cos_ref[...] = jnp.cos(angles)
@@ -184,9 +174,25 @@
     kv[z, y, D:KROWS] = p_rows
     kv[z, y, KROWS:KROWS + HALF] = v_lo.astype(BF16)
     kv[z, y, KROWS + HALF:KROWS + D] = v_hi.astype(BF16)
-    send("Y", kv.at[z, y], kv.at[z, y], partner)
-    for way in "RL":
-        send(f"Z{way}10", kv.at[z, y], kv.at[z, y], side[way][0])
+    pl.semaphore_wait(barrier, len(all_peers))
+
+    def kv_part(zz, yy, h):
+        return kv.at[zz, yy, pl.ds(0, KROWS) if h == 0 else pl.ds(KROWS, D)]
+
+    for h in (0, 1):
+        part = kv_part(z, y, h)
+        send(f"Y{h}", part, part, partner)
+        for way in "RL":
+            send(f"Z{way}10{h}", part, part, side[way][0])
+
+    for h in range(HEADS):
+        rows = slice(h * HALF, (h + 1) * HALF)
+        lo, hi = halves(g_ref[:, h * D:(h + 1) * D].astype(F32))
+        gc[x, rows, 0:D] = lo.astype(BF16)
+        gc[x, rows, D:] = hi.astype(BF16)
+
+    send("GL", gc.at[x], gc.at[x], left_x)
+    send("GR", gc.at[x], gc.at[x], right_x)
 
     for h in range(HEADS):
         rows = slice(h * HALF, (h + 1) * HALF)
@@ -226,19 +232,22 @@
         sums[0, 2 + part] = both[rows].reshape(8, 8, Q).sum(0)
 
     def kv_progress(r, d):
-        for way in "RL":
-            to, sign = side[way]
-            if d == 4 and r != last[way]:
-                continue
-            block = kv.at[zm(sign * d), ys[r]]
-            arrived(f"Z{way}{d}{r}", block)
-            if d < 3 or (d == 3 and r == last[way]):
-                send(f"Z{way}{d + 1}{r}", block, block, to)
+        for h in (0, 1):
+            for way in "RL":
+                to, sign = side[way]
+                if d == 4 and r != last[way]:
+                    continue
+                part = kv_part(zm(sign * d), ys[r], h)
+                arrived(f"Z{way}{d}{r}{h}", part)
+                if d < 3 or (d == 3 and r == last[way]):
+                    send(f"Z{way}{d + 1}{r}{h}", part, part, to)
 
     def y_progress():
-        arrived("Y", kv.at[z, ys[1]])
-        for way in "RL":
-            send(f"Z{way}11", kv.at[z, ys[1]], kv.at[z, ys[1]], side[way][0])
+        for h in (0, 1):
+            part = kv_part(z, ys[1], h)
+            arrived(f"Y{h}", part)
+            for way in "RL":
+                send(f"Z{way}11{h}", part, part, side[way][0])
 
     def gradient_forward():
         arrived("GL", gc.at[xm(1)])
@@ -408,7 +417,7 @@
         dvacc[k, :, 0:HALF] += dva + dvc[..., 0:D] * e1
         dvacc[k, :, HALF:] += dvc[..., D:] * (1.0 - e1)
 
-    def reduce_step(k):
+    def pair_done(k):
         for place, zz in enumerate((zm(k), zm(-k - 1))):
             if zz is zpos[0]:
                 continue
@@ -419,19 +428,16 @@
             for wi, way in enumerate("RL"):
                 r = last[way]
                 send(f"S{way}1{r}", dkv.at[zm(4), ys[r]], ring.at[wi, 0, r], side[way][0])
-            return
-        off = k + 1
-        step = 4 - off
-        for r in (0, 1):
-            for wi, way in enumerate("RL"):
-                zz = zm(off if way == "R" else -off)
-                part = dkv.at[zz, ys[r]]
-                if step > 1 or r == last[way]:
-                    came = ring.at[wi, step - 1, r]
-                    arrived(f"S{way}{step}{r}", came)
-                    part[...] = (part[...].astype(F32) + came[...].astype(F32)).astype(BF16)
-                send(f"S{way}{step + 1}{r}", part, ring.at[wi, step, r], side[way][0])
-
+
+    def ring_step(step, r):
+        off = 4 - step
+        for wi, way in enumerate("RL"):
+            part = dkv.at[zm(off if way == "R" else -off), ys[r]]
+            if step > 1 or r == last[way]:
+                came = ring.at[wi, step - 1, r]
+                arrived(f"S{way}{step}{r}", came)
+                part[...] = (part[...].astype(F32) + came[...].astype(F32)).astype(BF16)
+            send(f"S{way}{step + 1}{r}", part, ring.at[wi, step, r], side[way][0])
 
     def queries_out(m):
         dqs[m - 1] = dqacc[m].astype(BF16)
@@ -450,7 +456,10 @@
         for case in range(4):
             @pl.when(i == 3 * case + 6)
             def _(case=case):
-                reduce_step(3 - case)
+                pair_done(3 - case)
+                if case == 2:
+                    ring_step(1, 1)
+                    ring_step(1, 0)
         return carry
 
     lax.fori_loop(0, 16, second_loop, 0)
@@ -552,15 +561,15 @@
             total = total + ring[wi, 3, r].astype(F32)
         return total
 
-    for r in (1, 0):
-        for way in "RL":
-            wi = 0 if way == "R" else 1
+    def ring_end(r):
+        for wi, way in enumerate("RL"):
             arrived(f"S{way}4{r}", ring.at[wi, 3, r])
-        if r == 1:
-            ysend[...] = own_sum(1).astype(BF16)
-            send("SY", ysend, yrecv, partner)
-
+
+    ring_step(2, 1)
+    ring_step(2, 0)
+    ring_step(3, 1)
     copies = gain_start(1, gain_finish(0, copies))
+    ring_step(3, 0)
 
     def stored(lo, hi):
         return jnp.concatenate(
@@ -577,14 +586,19 @@
         whole = whole + dqr[m - 1].astype(F32)
     turned = jnp.transpose(whole) * SCALE
     for h in range(HEADS):
+        if h == 2:
+            ring_end(1)
+            ysend[...] = own_sum(1).astype(BF16)
+            send("SY", ysend, yrecv, partner)
+        if h == 5:
+            copies = gain_start(2, gain_finish(1, copies))
         cols = slice(h * D, (h + 1) * D)
         rows = slice(h * HALF, (h + 1) * HALF)
         gq = unrope(stored(turned[rows, 0:D], turned[rows, D:]))
         qn, inverse = normed(q_ref[:, cols].astype(F32))
         dq_ref[:, cols] = norm_back(gq, qn, inverse, qg_ref[...]).astype(BF16)
 
-    copies = gain_start(2, gain_finish(1, copies))
-
+    ring_end(0)
     arrived("SY", yrecv)
     own = own_sum(0) + yrecv[...].astype(F32)
     gk = unrope(stored(own[:HALF], own[HALF:D]))
@@ -592,10 +606,21 @@
     dk_ref[...] = norm_back(gk, kn, inverse, kg_ref[...]).astype(BF16)
     dv_ref[...] = stored(own[D:D + HALF], own[D + HALF:]).astype(BF16)
 
-    gain_ref[...] = gain_finish(2, copies)
+    total = gain_finish(2, copies)
+    qgain_ref[...] = total[0:1]
+    kgain_ref[...] = total[1:2]
 
     for name, src, dst, to in started:
         copy(name, src, dst, to).wait_send()
+
+
+def place(*refs):
+    sems = refs[-1]
+    copies = [pltpu.make_async_copy(refs[i], refs[5 + i], sems.at[i]) for i in range(5)]
+    for c in copies:
+        c.start()
+    for c in copies:
+        c.wait()
 
 
 def shards(heads_axis, query_raw, key_before_norm, values, grads, q_gain, k_gain, tok_pos):
@@ -603,16 +628,18 @@
     frequency = jnp.asarray(np.tile(frequency.astype(np.float32), 2).reshape(1, D))
     vmem = pl.BlockSpec(memory_space=pltpu.VMEM)
     count = len(MSG)
-    dq, dk, dv, gains = pl.pallas_call(
+    shapes = (
+        jax.ShapeDtypeStruct((D, HEADS * D), BF16),
+        jax.ShapeDtypeStruct((D, D), BF16),
+        jax.ShapeDtypeStruct((D, D), BF16),
+        jax.ShapeDtypeStruct((1, D), F32),
+        jax.ShapeDtypeStruct((1, D), F32),
+    )
+    results = pl.pallas_call(
         functools.partial(body, heads_axis),
-        out_shape=(
-            jax.ShapeDtypeStruct((D, HEADS * D), BF16),
-            jax.ShapeDtypeStruct((D, D), BF16),
-            jax.ShapeDtypeStruct((D, D), BF16),
-            jax.ShapeDtypeStruct((8, D), F32),
-        ),
+        out_shape=shapes,
         in_specs=[vmem] * 8,
-        out_specs=(vmem,) * 4,
+        out_specs=(vmem,) * 5,
         scratch_shapes=[
             pltpu.VMEM((D, D), F32),
             pltpu.VMEM((D, D), F32),
@@ -656,7 +683,15 @@
         query_raw, key_before_norm, values, grads,
         q_gain.reshape(1, D), k_gain.reshape(1, D), tok_pos.reshape(1, D), frequency,
     )
-    return dq, dk, dv, gains[0], gains[1]
+    anywhere = pl.BlockSpec(memory_space=pl.ANY)
+    dq, dk, dv, query_gain, key_gain = pl.pallas_call(
+        place,
+        out_shape=shapes,
+        in_specs=[vmem] * 5,
+        out_specs=(anywhere,) * 5,
+        scratch_shapes=[pltpu.SemaphoreType.DMA((5,))],
+    )(*results)
+    return dq, dk, dv, query_gain.reshape(D), key_gain.reshape(D)
 
 
 def solution(mesh):

time: 89.1 us -> 78.9 us (0.89)
  Pallas kernels: 83.9 us -> 78.1 us
  local copies, waits for them, and re-layouts: 4.33 us -> 0 us
    pallas_call x1 -> x2, Pallas kernels: 83.9 us -> 78.1 us  [the longest x1 76.3 us: shards(): pl.pallas_call(functools.partial(body, heads_axis), out_shape=shapes, in_...]
    unnamed x7 -> x0, local copies, waits for them, and re-layouts: 3.06 us -> none
    squeeze x1 -> x0, local copies, waits for them, and re-layouts: 1.27 us -> none  [shards(): return (dq, dk, dv, gains[0], gains[1])]
where the time goes in v5:
time: 78.9 us; the launch traced here: 78.7 us
  Pallas kernels  78.1 us (99%)
    pallas_call x1, Pallas kernels, shards(): pl.pallas_call(functools.partial(body, heads_axis), out_shape=shapes, in_...  76.3 us
    pallas_call x1, Pallas kernels, shards(): pl.pallas_call(place, out_shape=shapes, in_specs=[vmem] * 5, out_specs=(a...  1.74 us

profile of v5, /device:TPU:1, one launch (start us, length us, event | category | flops | bytes accessed | tf_op | source)
XLA Modules:
  0.0 78.7 jit_solution(2035810352189525241)
XLA Ops:
  0.6 76.3 %shard_map.119 = (bf16[128,1024]{1,0:T(8,128)(2,1)}, bf16[128,128]{1,0:T(8,128)(2,1)}, bf16[128,128]{1,0:T(8,128)(2,1)}, f32[1,128]{1,0:T(1,128)}, f32[1,128]{1,0:T(1,128)}) custom-call(bf16[128,1024]{1,0:T(8,128)(2,1)} %q_ref.1, bf16[128,128]{1,0:T(8,128)(2,1)} %k_ref.1, bf16[128,128]{1,0:T(8,128)(2,1)} %v_ref.1, bf16[128,1024]{1,0:T(8,128)(2,1)} %g_ref.1, ...), custom_call_target="tpu_custom_call" | custom-call | tf_op jit(solution)/shard_map/pallas_call | solution.py:638
  77.0 1.7 %shard_map.120 = (bf16[128,1024]{1,0:T(8,128)(2,1)}, bf16[128,128]{1,0:T(8,128)(2,1)}, bf16[128,128]{1,0:T(8,128)(2,1)}, f32[1,128]{1,0:T(1,128)}, f32[1,128]{1,0:T(1,128)}) custom-call(bf16[128,1024]{1,0:T(8,128)(2,1)} %get-tuple-element.15.refs_0_, bf16[128,128]{1,0:T(8,128)(2,1)} %get-tuple-element.16.refs_1_, ...), custom_call_target="tpu_custom_call" | custom-call | tf_op jit(solution)/shard_map/pallas_call | solution.py:687

commit v6 on v5

--- a/solution.py
+++ b/solution.py
@@ -367,6 +367,12 @@
 
     lax.fori_loop(0, X, query_tables, 0)
 
+    for k in range(4):
+        dkacc[k] = jnp.zeros((4, D, D), F32)
+        dvacc[k] = jnp.zeros((4, D, D), F32)
+    for m in (1, 2, 3):
+        dqacc[m] = jnp.zeros((2 * D, Q), F32)
+
     for j in range(4):
         for m in (1, 2, 3):
             arrived(f"ST{j}{m}", stbuf.at[xm(rel_of(j) - m), xm(-m)])
@@ -382,15 +388,10 @@
     gs = (pr * (g_d[...] - jnp.where(rowsel, stats[x, 2:3], stats[x, 3:4]))).astype(BF16)
     pr = pr.astype(BF16)
     top = lax.broadcasted_iota(jnp.int32, (D, D), 0) < HALF
-    for k in range(4):
-        dkacc[k] = jnp.zeros((4, D, D), F32)
-        dvacc[k] = jnp.zeros((4, D, D), F32)
     full = dot(pr, gc[x], NN)
     dvacc[0, y] = jnp.where(top, full[:, 0:D], full[:, D:])
     full = dot(gs, qc[x, 0:Q], NN)
     dkacc[0, y] = jnp.where(top, full[:, 0:D], full[:, D:])
-    for m in (1, 2, 3):
-        dqacc[m] = jnp.zeros((2 * D, Q), F32)
     dqacc[0] = dot(own_k(), gs, TN)
 
     def pass_two(k, b, rel, u):
@@ -444,25 +445,27 @@
         send(f"DQ{m}", dqs.at[m - 1], dqr.at[m - 1], xdev[m])
 
     def second_loop(i, carry):
-        near = (i + 12) // 16
-        k = (1 - near) * (3 - i) + near * (3 - (i + 8) // 3 + 4)
-        j = (1 - near) * 3 + near * (2 - (i + 8) % 3)
+        a, c = (i + 12) // 16, (i + 9) // 16
+        k = (1 - a) * 3 + (a - c) * (6 - i) + c * (5 - (i + 2) // 3)
+        j = (1 - a) * (3 - i) + (a - c) * 3 + c * (2 - (i + 2) % 3)
         rel = rel_of(j)
         pass_two(k, lax.rem(x + rel, X), rel, k * 4 + rel)
-        for case, m in ((3, 2), (13, 3), (14, 1)):
+        for case, m in ((6, 2), (13, 3), (14, 1)):
             @pl.when(i == case)
             def _(m=m):
                 queries_out(m)
         for case in range(4):
-            @pl.when(i == 3 * case + 6)
+            @pl.when(i == (3 if case == 0 else 3 * case + 6))
             def _(case=case):
                 pair_done(3 - case)
-                if case == 2:
+                if case == 1:
                     ring_step(1, 1)
                     ring_step(1, 0)
         return carry
 
     lax.fori_loop(0, 16, second_loop, 0)
+
+    ring_step(2, 1)
 
     first_lanes = lax.broadcasted_iota(jnp.int32, (1, D), 1) < HALF
 
@@ -565,7 +568,6 @@
         for wi, way in enumerate("RL"):
             arrived(f"S{way}4{r}", ring.at[wi, 3, r])
 
-    ring_step(2, 1)
     ring_step(2, 0)
     ring_step(3, 1)
     copies = gain_start(1, gain_finish(0, copies))

time: 78.9 us -> 78.2 us (level)
  no operation moved by 1% of the time
where the time goes in v6:
time: 78.2 us; the launch traced here: 78 us
  Pallas kernels  77.4 us (99%)
    pallas_call x1, Pallas kernels, shards(): pl.pallas_call(functools.partial(body, heads_axis), out_shape=shapes, in_...  75.6 us
    pallas_call x1, Pallas kernels, shards(): pl.pallas_call(place, out_shape=shapes, in_specs=[vmem] * 5, out_specs=(a...  1.74 us

profile of v6, /device:TPU:1, one launch (start us, length us, event | category | flops | bytes accessed | tf_op | source)
XLA Modules:
  0.0 78.0 jit_solution(186073520271609563)
XLA Ops:
  0.6 75.6 %shard_map.119 = (bf16[128,1024]{1,0:T(8,128)(2,1)}, bf16[128,128]{1,0:T(8,128)(2,1)}, bf16[128,128]{1,0:T(8,128)(2,1)}, f32[1,128]{1,0:T(1,128)}, f32[1,128]{1,0:T(1,128)}) custom-call(bf16[128,1024]{1,0:T(8,128)(2,1)} %q_ref.1, bf16[128,128]{1,0:T(8,128)(2,1)} %k_ref.1, bf16[128,128]{1,0:T(8,128)(2,1)} %v_ref.1, bf16[128,1024]{1,0:T(8,128)(2,1)} %g_ref.1, ...), custom_call_target="tpu_custom_call" | custom-call | tf_op jit(solution)/shard_map/pallas_call | solution.py:640
  76.3 1.7 %shard_map.120 = (bf16[128,1024]{1,0:T(8,128)(2,1)}, bf16[128,128]{1,0:T(8,128)(2,1)}, bf16[128,128]{1,0:T(8,128)(2,1)}, f32[1,128]{1,0:T(1,128)}, f32[1,128]{1,0:T(1,128)}) custom-call(bf16[128,1024]{1,0:T(8,128)(2,1)} %get-tuple-element.15.refs_0_, bf16[128,128]{1,0:T(8,128)(2,1)} %get-tuple-element.16.refs_1_, ...), custom_call_target="tpu_custom_call" | custom-call | tf_op jit(solution)/shard_map/pallas_call | solution.py:689

commit v7 on v6

--- a/solution.py
+++ b/solution.py
@@ -582,16 +582,15 @@
         s = g * gain
         return inverse * (s - xn * jnp.mean(s * xn, axis=-1, keepdims=True))
 
+    ring_end(1)
+    ysend[...] = own_sum(1).astype(BF16)
+    send("SY", ysend, yrecv, partner)
     whole = dqacc[0]
     for m in (1, 2, 3):
         arrived(f"DQ{m}", dqr.at[m - 1])
         whole = whole + dqr[m - 1].astype(F32)
     turned = jnp.transpose(whole) * SCALE
     for h in range(HEADS):
-        if h == 2:
-            ring_end(1)
-            ysend[...] = own_sum(1).astype(BF16)
-            send("SY", ysend, yrecv, partner)
         if h == 5:
             copies = gain_start(2, gain_finish(1, copies))
         cols = slice(h * D, (h + 1) * D)

time: 78.2 us -> 78.2 us (level)
  no operation moved by 1% of the time
where the time goes in v7:
time: 78.2 us; the launch traced here: 78 us
  Pallas kernels  77.4 us (99%)
    pallas_call x1, Pallas kernels, shards(): pl.pallas_call(functools.partial(body, heads_axis), out_shape=shapes, in_...  75.6 us
    pallas_call x1, Pallas kernels, shards(): pl.pallas_call(place, out_shape=shapes, in_specs=[vmem] * 5, out_specs=(a...  1.74 us

profile of v7, /device:TPU:1, one launch (start us, length us, event | category | flops | bytes accessed | tf_op | source)
XLA Modules:
  0.0 78.0 jit_solution(12120541535616783409)
XLA Ops:
  0.6 75.6 %shard_map.119 = (bf16[128,1024]{1,0:T(8,128)(2,1)}, bf16[128,128]{1,0:T(8,128)(2,1)}, bf16[128,128]{1,0:T(8,128)(2,1)}, f32[1,128]{1,0:T(1,128)}, f32[1,128]{1,0:T(1,128)}) custom-call(bf16[128,1024]{1,0:T(8,128)(2,1)} %q_ref.1, bf16[128,128]{1,0:T(8,128)(2,1)} %k_ref.1, bf16[128,128]{1,0:T(8,128)(2,1)} %v_ref.1, bf16[128,1024]{1,0:T(8,128)(2,1)} %g_ref.1, ...), custom_call_target="tpu_custom_call" | custom-call | tf_op jit(solution)/shard_map/pallas_call | solution.py:639
  76.3 1.7 %shard_map.120 = (bf16[128,1024]{1,0:T(8,128)(2,1)}, bf16[128,128]{1,0:T(8,128)(2,1)}, bf16[128,128]{1,0:T(8,128)(2,1)}, f32[1,128]{1,0:T(1,128)}, f32[1,128]{1,0:T(1,128)}) custom-call(bf16[128,1024]{1,0:T(8,128)(2,1)} %get-tuple-element.15.refs_0_, bf16[128,128]{1,0:T(8,128)(2,1)} %get-tuple-element.16.refs_1_, ...), custom_call_target="tpu_custom_call" | custom-call | tf_op jit(solution)/shard_map/pallas_call | solution.py:688
